TPU v7x, 256 devices: a whole 4x4x8 slice. The times are simulated.
256 devices in a mesh: dp: 32 (over x, y, core), tensor: 8 (over z).
Axes of the slice: x: 4, y: 4, z: 8, core: 2. Of those that a mesh axis runs over, the one named last changes fastest.
Arguments:
- grads: bfloat16 [2, 32, 8192, 512], P(None, 'dp', 'tensor'), may hold values from -48 to 48
- errors: float32 [2, 32, 8192, 512], P(None, 'dp', 'tensor'), may hold values from -6 to 6
- q_prev: float32 [2, 512, 32], replicated, may hold values from -6 to 6
Outputs:
- decompressed: bfloat16 [2, 8192, 512], P(None, 'tensor')
- new_errors: float32 [2, 32, 8192, 512], P(None, 'dp', 'tensor')
- q_new: float32 [2, 512, 32], replicated
All inputs are finite; a program needn't handle non-finite values.
Results may differ from a plain program's by a relative error of at most 0.001.
Values sent between devices are 32-bit elements; how exact they have to be, the bound alone decides.
No kernel may reach another device: no remote copies, remote signals or barrier semaphores. Data moves between devices by JAX's collectives and lax.ppermute only.
A program may use at most 64 MiB of HBM per device.

v0:
```python
import jax
import jax.numpy as jnp
from jax import lax
from jax.sharding import PartitionSpec as P

highest = lax.Precision.HIGHEST


def by_gram(factor, summer):
    gram = summer(jnp.einsum("lrk,lrm->lkm", factor, factor, precision=highest))
    lower = jnp.linalg.cholesky(gram)
    return lax.linalg.triangular_solve(lower, factor, left_side=False, lower=True, transpose_a=True)


def on_device(grads, errors, q_prev):
    replicas = lax.axis_size("dp")
    merged = grads[:, 0].astype(jnp.float32) + errors[:, 0]
    left_term = jnp.einsum("lrc,lck->lrk", merged, q_prev, precision=highest)
    factor = lax.psum(left_term, "dp") / replicas
    p_hat = by_gram(factor, lambda gram: lax.psum(gram, "tensor"))
    right_term = jnp.einsum("lrc,lrk->lck", merged, p_hat, precision=highest)
    right = lax.psum(right_term, ("dp", "tensor")) / replicas
    approx = jnp.einsum("lrk,lck->lrc", p_hat, right, precision=highest)
    return (approx.astype(jnp.bfloat16), (merged - approx)[:, None], right)


def solution(mesh):
    placed = (P(None, "dp", "tensor", None), P(None, "dp", "tensor", None), P())
    return jax.shard_map(
        on_device,
        mesh=mesh,
        in_specs=placed,
        out_specs=(P(None, "tensor", None), P(None, "dp", "tensor", None), P()),
        check_vma=False,
    )
```

profile of v0, /device:TPU:1, one launch (start us, length us, event | category | flops | bytes accessed | tf_op | source)
XLA Modules:
  0.0 433.3 jit_solution(13377600207712736178)
XLA Ops:
  7.2 0.0 copy-start
  7.2 0.0 copy-start.1
  7.2 0.0 all-reduce.3.cloned.1.call-start
  7.2 0.8 copy-done
  8.1 7.6 %fusion.2 = f32[2,1024,32]{1,2,0:T(8,128)} fusion(f32[2,512,32]{1,2,0:T(8,128)S(1)} %copy-done, f32[2,1,1024,512]{3,2,1,0:T(8,128)} %param.4, bf16[2,1,1024,512]{3,2,1,0:T(8,128)(2,1)} %param.3), kind=kOutput, calls=%fused_computation.3 | convolution fusion | flops 404750336 | bytes 6684672 | tf_op jit(solution)/shard_map/lrc,lck->lrk/dot_general | solution.py:18
  15.7 0.0 all-reduce.3.cloned.1.call-update
  15.7 0.0 all-reduce.5.cloned.1.call-start
  15.8 115.2 %all-reduce.3.cloned.1.call-done = f32[2,1024,32]{1,2,0:T(8,128)} async-done(((f32[2,1024,32]{1,2,0:T(8,128)}), f32[2,1024,32]{1,2,0:T(8,128)}) %all-reduce.3.cloned.1.call-update) | async-done | bytes 262160 | tf_op jit(solution)/shard_map/psum | solution.py:19
  131.0 1.4 fusion.7
  132.4 23.0 %psum.22 = f32[2,32,32]{1,2,0:T(8,128)S(1)} all-reduce(f32[2,32,32]{1,2,0:T(8,128)S(1)} %fusion.7), channel_id=1, replica_groups=mesh['dp'=32,'tensor'=8] {'tensor'}, use_global_device_ids=true, to_apply=%region_1.0 | all-reduce | flops 2048 | bytes 16384 | tf_op jit(solution)/shard_map/psum | solution.py:20
  155.4 0.1 copy.15
  155.4 5.9 %custom-call.7 = f32[2,32,32]{2,1,0:T(8,128)S(1)} custom-call(f32[2,32,32]{2,1,0:T(8,128)S(1)} %fusion.12), custom_call_target="Cholesky" | custom-call | tf_op jit(solution)/shard_map/jit(cholesky)/cholesky | solution.py:11
  161.3 0.1 compare_reduce_fusion
  161.5 0.1 select_bitcast_fusion
  161.5 4.9 %custom-call.8 = f32[2,1,32,32]{2,3,1,0:T(8,128)S(1)} custom-call(f32[2,1,32,32]{3,2,1,0:T(8,128)S(1)} %select_bitcast_fusion), custom_call_target="InvertDiagBlocksLowerTriangular" | custom-call | tf_op jit(solution)/shard_map/triangular_solve | solution.py:12
  166.5 1.4 fusion.5
  167.8 0.0 copy-done.1
  167.9 5.6 %fusion = f32[2,512,32]{1,2,0:T(8,128)} fusion(f32[2,1024,32]{1,2,0:T(8,128)S(1)} %fusion.5, f32[2,1,1024,512]{3,2,1,0:T(8,128)} %param.4, bf16[2,1,1024,512]{3,2,1,0:T(8,128)(2,1)S(1)} %copy-done.1), kind=kOutput, calls=%fused_computation.1 | convolution fusion | flops 404750336 | bytes 6684672 | tf_op jit(solution)/shard_map/lrc,lrk->lck/dot_general | solution.py:21
  173.5 0.0 all-reduce.5.cloned.1.call-update
  173.5 244.8 %all-reduce.5.cloned.1.call-done = f32[2,512,32]{1,2,0:T(8,128)} async-done(((f32[2,512,32]{1,2,0:T(8,128)}), f32[2,512,32]{1,2,0:T(8,128)}) %all-reduce.5.cloned.1.call-update) | async-done | bytes 131088 | tf_op jit(solution)/shard_map/psum | solution.py:22
  418.2 0.9 broadcast_multiply_fusion
  419.2 0.0 copy-start.2
  419.2 7.3 %fusion.4 = (f32[2,1,1024,512]{3,2,1,0:T(8,128)}, bf16[2,1024,512]{2,1,0:T(8,128)(2,1)}) fusion(f32[2,1,1024,512]{3,2,1,0:T(8,128)} %param.4, bf16[2,1,1024,512]{3,2,1,0:T(8,128)(2,1)S(1)} %copy-done.1, f32[2,1024,32]{1,2,0:T(8,128)S(1)} %fusion.5, f32[2,512,32]{1,2,0:T(8,128)S(1)} %broadcast_multiply_fusion), kind=kOutput, calls=%fused_computation.5 | convolution fusion | flops 406847488 | bytes 12976128 | tf_op jit(solution)/shard_map/lrk,lck->lrc/dot_general | solution.py:23
  426.4 0.0 copy-done.2
  (4 shorter events, 0.1 us)
Async XLA Ops:
  7.2 0.9 copy-start
  7.2 160.7 %copy-start.1 = (bf16[2,1,1024,512]{3,2,1,0:T(8,128)(2,1)S(1)}, bf16[2,1,1024,512]{3,2,1,0:T(8,128)(2,1)}, u32[]{:S(2)}) copy-start(bf16[2,1,1024,512]{3,2,1,0:T(8,128)(2,1)} %param.3) | copy-start | bytes 6291460
  7.2 123.8 %all-reduce.3.cloned.1.call-start = ((), (), s32[]{:S(2)}) async-start(), calls=%async_computation | async-start | bytes 524288 | tf_op jit(solution)/shard_map/psum | solution.py:19
  15.7 402.6 %all-reduce.5.cloned.1.call-start = ((), (), s32[]{:S(2)}) async-start(), calls=%async_computation.1 | async-start | bytes 262144 | tf_op jit(solution)/shard_map/psum | solution.py:22
  419.2 7.3 %copy-start.2 = (f32[2,512,32]{1,2,0:T(8,128)}, f32[2,512,32]{1,2,0:T(8,128)S(1)}, u32[]{:S(2)}) copy-start(f32[2,512,32]{1,2,0:T(8,128)S(1)} %broadcast_multiply_fusion) | copy-start | bytes 393220
Sparse Core Ops, SparseCore 0:
  15.8 115.1 all-reduce.2
  173.6 244.5 all-reduce.4
where the time goes:
time: 434 us; the launch traced here: 433 us
  waiting for transfers between devices  360 us (83%)
  matrix products  23.2 us (5%)
  blocking collectives  23 us (5%)
  between operations  14.1 us (3%)
  other arithmetic  11.9 us (3%)
    psum x1, waiting for transfers between devices, on_device(): right = lax.psum(right_term, ('dp', 'tensor')) / replicas  245 us
    psum x1, waiting for transfers between devices, on_device(): factor = lax.psum(left_term, 'dp') / replicas  115 us
    psum x1, blocking collectives, on_device(): p_hat = by_gram(factor, lambda gram: lax.psum(gram, 'tensor'))  23 us
  transfers between devices with their start and end apart: 2, of which 2 were waited for; matrix products, arithmetic and copies ran while one was open for 0% of the time, Pallas kernels for 0%

commit v1 on v0

v1 whole, which is shorter than its diff:
```python
import jax
import jax.numpy as jnp
from jax import lax
from jax.experimental import pallas as pl
from jax.experimental.pallas import tpu as pltpu
from jax.sharding import PartitionSpec as P

highest = lax.Precision.HIGHEST
f32, bf16 = jnp.float32, jnp.bfloat16
block_rows = 256


def halves(x):
    high = x.astype(bf16)
    return high, (x - high.astype(f32)).astype(bf16)


def thirds(x):
    high = x.astype(bf16)
    rest = x - high.astype(f32)
    return high, *halves(rest)


def dot(a, b, contract, precision=None):
    return lax.dot_general(a, b, (contract, ((), ())), precision=precision, preferred_element_type=f32)


def split_dot(small, high, low, contract):
    rows = small.shape[0]
    one, two, three = thirds(small)
    by_high = dot(jnp.concatenate([one, two, three], 0), high, contract)
    by_low = dot(jnp.concatenate([one, two], 0), low, contract)
    small_terms = by_high[rows : 2 * rows] + by_low[:rows]
    tiny_terms = by_high[2 * rows :] + by_low[rows:]
    return by_high[:rows] + (small_terms + tiny_terms)


def left_kernel(grads, errors, q_t, high, low, part):
    merged = grads[0].astype(f32) + errors[0]
    merged_high, merged_low = halves(merged)
    high[0] = merged_high
    low[0] = merged_low
    term = split_dot(q_t[0], merged_high, merged_low, ((1,), (1,)))
    for at in range(part.shape[1]):
        part[0, at] = term[:, at * 128 : (at + 1) * 128]


def left(grads, errors, q_t):
    layers, rows, cols = grads.shape
    rank = q_t.shape[1]
    lanes = block_rows // 128
    wide = pl.BlockSpec((1, block_rows, cols), lambda l, b: (l, b, 0))
    return pl.pallas_call(
        left_kernel,
        grid=(layers, rows // block_rows),
        in_specs=[wide, wide, pl.BlockSpec((1, rank, cols), lambda l, b: (l, 0, 0))],
        out_specs=[wide, wide, pl.BlockSpec((1, lanes, rank, 128), lambda l, b: (l, b, 0, 0))],
        out_shape=[
            jax.ShapeDtypeStruct(grads.shape, bf16),
            jax.ShapeDtypeStruct(grads.shape, bf16),
            jax.ShapeDtypeStruct((layers, rows // 128, rank, 128), f32),
        ],
        name="left",
    )(grads, errors, q_t)


def spread(x, scale):
    def kernel(x, out):
        total = jnp.sum(x[...], axis=0) * scale
        out[...] = jnp.broadcast_to(total[None], out.shape)

    return pl.pallas_call(kernel, out_shape=jax.ShapeDtypeStruct(x.shape, f32), name="spread")(x)


def right_kernel(high, low, p_t, raw, gram):
    rank = p_t.shape[2]
    factor = jnp.concatenate([p_t[0, at] for at in range(p_t.shape[1])], 1)
    term = split_dot(factor, high[0], low[0], ((1,), (0,)))
    square = dot(factor, factor, ((1,), (1,)), highest)
    packed = jnp.concatenate([square[at : at + 8] for at in range(0, rank, 8)], 1)

    @pl.when(pl.program_id(1) == 0)
    def _():
        for at in range(raw.shape[1]):
            raw[0, at] = term[:, at * 128 : (at + 1) * 128]
        gram[0] = packed

    @pl.when(pl.program_id(1) != 0)
    def _():
        for at in range(raw.shape[1]):
            raw[0, at] += term[:, at * 128 : (at + 1) * 128]
        gram[0] += packed


def right(high, low, p_t):
    layers, rows, cols = high.shape
    rank = p_t.shape[2]
    lanes = block_rows // 128
    wide = pl.BlockSpec((1, block_rows, cols), lambda l, b: (l, b, 0))
    return pl.pallas_call(
        right_kernel,
        grid=(layers, rows // block_rows),
        in_specs=[wide, wide, pl.BlockSpec((1, lanes, rank, 128), lambda l, b: (l, b, 0, 0))],
        out_specs=[
            pl.BlockSpec((1, cols // 128, rank, 128), lambda l, b: (l, 0, 0, 0)),
            pl.BlockSpec((1, 8, 128), lambda l, b: (l, 0, 0)),
        ],
        out_shape=[
            jax.ShapeDtypeStruct((layers, cols // 128, rank, 128), f32),
            jax.ShapeDtypeStruct((layers, 8, 128), f32),
        ],
        name="right",
    )(high, low, p_t)


def mix(raw, gram, copies):
    def kernel(raw, gram, out):
        total = jnp.sum(raw[...], axis=0)
        both = jnp.concatenate([total, gram[0], gram[1]], 0)
        out[...] = jnp.broadcast_to(both[None], out.shape)

    shape = (copies, raw.shape[1] + 16, 128)
    return pl.pallas_call(kernel, out_shape=jax.ShapeDtypeStruct(shape, f32), name="mix")(raw, gram)


def unmix(x, copies, scale):
    def kernel(x, piece, gram):
        total = jnp.sum(x[...], axis=0)
        piece[...] = jnp.broadcast_to(total[None, :8] * scale, piece.shape)
        gram[0] = total[8:16]
        gram[1] = total[16:24]

    return pl.pallas_call(
        kernel,
        out_shape=[jax.ShapeDtypeStruct((copies, 8, 128), f32), jax.ShapeDtypeStruct((2, 8, 128), f32)],
        name="unmix",
    )(x)


def orthonormal_kernel(gram, p_t, inverse, p_hat):
    layers, _, rank, _ = p_t.shape
    squares = [jnp.concatenate([gram[l][:, at : at + rank] for at in range(0, 128, rank)], 0) for l in range(layers)]
    row = lax.broadcasted_iota(jnp.int32, (rank, 128), 0)
    lane = lax.broadcasted_iota(jnp.int32, (rank, 128), 1)
    first = (lane // rank) % 2 == 0
    unit = (lane % rank == row).astype(f32)
    both = jnp.concatenate(squares + [unit[:, : 2 * rank]], 1)
    pivots = jnp.ones((rank, 128), f32)
    for k in range(rank):
        column = jnp.where(first, both[:, k : k + 1], both[:, rank + k : rank + k + 1])
        pivot = column[k : k + 1]
        pivots = jnp.where(row == k, pivot, pivots)
        if k < rank - 1:
            factor = jnp.where(row > k, column / pivot, 0.0)
            both = both - factor * both[k : k + 1]
    scaled = both / jnp.sqrt(pivots)
    for l in range(layers):
        lower_inverse = scaled[:, (2 + l) * rank : (3 + l) * rank]
        inverse[l] = lower_inverse
        for at in range(p_t.shape[1]):
            hat_t = dot(lower_inverse, p_t[l, at], ((1,), (0,)), highest)
            high = hat_t.astype(bf16).astype(f32)
            low = hat_t - high
            stack = jnp.concatenate([high, low, high, jnp.zeros_like(high)], 0)
            p_hat[l, at * 128 : (at + 1) * 128] = stack.T.astype(bf16)


def orthonormal(gram, p_t):
    layers, tiles, rank, _ = p_t.shape
    return pl.pallas_call(
        orthonormal_kernel,
        out_shape=[
            jax.ShapeDtypeStruct((layers, rank, rank), f32),
            jax.ShapeDtypeStruct((layers, tiles * 128, 4 * rank), bf16),
        ],
        cost_estimate=pl.CostEstimate(flops=400_000_000, bytes_accessed=1_000_000, transcendentals=0),
        name="orthonormal",
    )(gram, p_t)


def last_kernel(high, low, p_hat, inverse, raw, decompressed, new_errors, q_new, stack):
    @pl.when(pl.program_id(1) == 0)
    def _():
        whole = jnp.concatenate([raw[0, at] for at in range(raw.shape[1])], 1)
        q = dot(inverse[0], whole, ((1,), (0,)), highest)
        q_new[0] = q
        q_high, q_low = halves(q)
        stack[...] = jnp.concatenate([q_high, q_high, q_low, jnp.zeros_like(q_high)], 0)

    approx = dot(p_hat[0], stack[...], ((1,), (0,)))
    decompressed[0] = approx.astype(bf16)
    new_errors[0] = (high[0].astype(f32) + low[0].astype(f32)) - approx


def last(high, low, p_hat, inverse, raw):
    layers, rows, cols = high.shape
    rank = inverse.shape[1]
    wide = pl.BlockSpec((1, block_rows, cols), lambda l, b: (l, b, 0))
    return pl.pallas_call(
        last_kernel,
        grid=(layers, rows // block_rows),
        in_specs=[
            wide,
            wide,
            pl.BlockSpec((1, block_rows, 4 * rank), lambda l, b: (l, b, 0)),
            pl.BlockSpec((1, rank, rank), lambda l, b: (l, 0, 0)),
            pl.BlockSpec((1, cols // 128, rank, 128), lambda l, b: (l, 0, 0, 0)),
        ],
        out_specs=[wide, wide, pl.BlockSpec((1, rank, cols), lambda l, b: (l, 0, 0))],
        out_shape=[
            jax.ShapeDtypeStruct(high.shape, bf16),
            jax.ShapeDtypeStruct(high.shape, f32),
            jax.ShapeDtypeStruct((layers, rank, cols), f32),
        ],
        scratch_shapes=[pltpu.VMEM((4 * rank, cols), bf16)],
        name="last",
    )(high, low, p_hat, inverse, raw)


def exchange(x, axis):
    return lax.all_to_all(x, axis, 0, 0, tiled=True)


def on_device(grads, errors, q_prev):
    replicas, slabs = lax.axis_size("dp"), lax.axis_size("tensor")
    high, low, part = left(grads[:, 0], errors[:, 0], jnp.swapaxes(q_prev, 1, 2))
    tiles_shape = part.shape
    part = exchange(part.reshape(replicas, -1, 128), "dp")
    p_t = exchange(spread(part, 1.0 / replicas), "dp").reshape(tiles_shape)
    raw, gram = right(high, low, p_t)
    raw_shape = raw.shape
    raw = exchange(raw.reshape(replicas, -1, 128), "dp")
    both = exchange(mix(raw, gram, slabs), "tensor")
    raw, gram = unmix(both, replicas, 1.0 / replicas)
    raw = exchange(raw, "dp").reshape(raw_shape)
    inverse, p_hat = orthonormal(gram, p_t)
    decompressed, new_errors, q_new = last(high, low, p_hat, inverse, raw)
    return decompressed, new_errors[:, None], jnp.swapaxes(q_new, 1, 2)


def solution(mesh):
    placed = (P(None, "dp", "tensor", None), P(None, "dp", "tensor", None), P())
    return jax.shard_map(
        on_device,
        mesh=mesh,
        in_specs=placed,
        out_specs=(P(None, "tensor", None), P(None, "dp", "tensor", None), P()),
        check_vma=False,
    )
```

time: 434 us -> 101 us (0.23)
  waiting for transfers between devices: 360 us -> 2.68 us
  blocking collectives: 23 us -> 59.1 us
  Pallas kernels: 0 us -> 31.8 us
  matrix products: 23.2 us -> 0 us
  between operations: 14.1 us -> 0.65 us
  other arithmetic: 11.9 us -> 0 us
  starting transfers between devices: 0.08 us -> 5.51 us
    psum x2 -> x0, waiting for transfers between devices: 360 us -> none  [the longest x1 245 us: on_device(): right = lax.psum(right_term, ('dp', 'tensor')) / replicas]
    all_to_all x0 -> x4, blocking collectives: none -> 59.1 us  [exchange(): return lax.all_to_all(x, axis, 0, 0, tiled=True)]
    pallas_call x0 -> x7, Pallas kernels: none -> 31.8 us  [the longest x1 8.07 us: last(): pl.pallas_call(last_kernel, grid=(layers, rows // block_rows), in_specs=[...]
    psum x1 -> x0, blocking collectives: 23 us -> none  [on_device(): p_hat = by_gram(factor, lambda gram: lax.psum(gram, 'tensor'))]
    dot_general x4 -> x0, matrix products: 21.9 us -> none  [the longest x1 7.59 us: on_device(): left_term = jnp.einsum('lrc,lck->lrk', merged, q_prev, precision=highest)]
    another operation x7 -> x0, other arithmetic: 11 us -> none  [the longest x4 6.03 us: by_gram(): lower = jnp.linalg.cholesky(gram)]
    all_to_all x0 -> x1, starting transfers between devices: none -> 5.51 us  [exchange(): return lax.all_to_all(x, axis, 0, 0, tiled=True)]
  transfers between devices with their start and end apart: 2 -> 1, of which waited for: 2 -> 1; matrix products, arithmetic and copies ran while one was open for 0% -> 0% of each run, Pallas kernels for 0% -> 5%
where the time goes in v1:
time: 101 us; the launch traced here: 100 us
  blocking collectives  59.1 us (59%)
  Pallas kernels  31.8 us (31%)
  starting transfers between devices  5.51 us (5%)
  waiting for transfers between devices  2.68 us (3%)
    all_to_all x4, blocking collectives, exchange(): return lax.all_to_all(x, axis, 0, 0, tiled=True)  59.1 us
    pallas_call x1, Pallas kernels, last(): pl.pallas_call(last_kernel, grid=(layers, rows // block_rows), in_specs=[...  8.07 us
    pallas_call x1, Pallas kernels, left(): pl.pallas_call(left_kernel, grid=(layers, rows // block_rows), in_specs=[...  7.33 us
    pallas_call x1, Pallas kernels, right(): pl.pallas_call(right_kernel, grid=(layers, rows // block_rows), in_specs=...  6.46 us
    all_to_all x1, starting transfers between devices, exchange(): return lax.all_to_all(x, axis, 0, 0, tiled=True)  5.51 us
    pallas_call x1, Pallas kernels, orthonormal(): pl.pallas_call(orthonormal_kernel, out_shape=[jax.ShapeDtypeStruct((layer...  5.14 us
    all_to_all x1, waiting for transfers between devices, exchange(): return lax.all_to_all(x, axis, 0, 0, tiled=True)  2.68 us
  transfers between devices with their start and end apart: 1, of which 1 were waited for; matrix products, arithmetic and copies ran while one was open for 0% of the time, Pallas kernels for 5%

profile of v1, /device:TPU:1, one launch (start us, length us, event | category | flops | bytes accessed | tf_op | source)
XLA Modules:
  0.0 100.4 jit_solution(3872606762567232805)
XLA Ops:
  0.6 7.3 %left.1 = (bf16[2,1024,512]{2,1,0:T(8,128)(2,1)}, bf16[2,1024,512]{2,1,0:T(8,128)(2,1)}, f32[2,8,32,128]{3,2,1,0:T(8,128)}) custom-call(bf16[2,1024,512]{2,1,0:T(8,128)(2,1)} %bitcast.12, f32[2,1024,512]{2,1,0:T(8,128)} %bitcast.11, f32[2,32,512]{2,1,0:T(8,128)} %bitcast.17), custom_call_target="tpu_custom_call" | custom-call | tf_op jit(solution)/shard_map/left/pallas_call | solution.py:53
  8.0 17.7 %all_to_all.25.x = f32[32,16,128]{2,1,0:T(8,128)} all-to-all(f32[32,16,128]{2,1,0:T(8,128)} %bitcast.16), channel_id=1, replica_groups=mesh['dp'=32,'tensor'=8] {'dp'}, dimensions={0} | all-to-all | bytes 524288 | tf_op jit(solution)/shard_map/all_to_all | solution.py:221
  25.6 1.7 %spread.1 = f32[32,16,128]{2,1,0:T(8,128)} custom-call(f32[32,16,128]{2,1,0:T(8,128)} %all_to_all.25.x), custom_call_target="tpu_custom_call" | custom-call | tf_op jit(solution)/shard_map/spread/pallas_call | solution.py:72
  27.3 13.5 %all_to_all.26 = f32[32,16,128]{2,1,0:T(8,128)} all-to-all(f32[32,16,128]{2,1,0:T(8,128)} %spread.1), channel_id=1, replica_groups=mesh['dp'=32,'tensor'=8] {'dp'}, dimensions={0} | all-to-all | bytes 524288 | tf_op jit(solution)/shard_map/all_to_all | solution.py:221
  40.8 6.5 %right.1 = (f32[2,4,32,128]{3,2,1,0:T(8,128)}, f32[2,8,128]{2,1,0:T(8,128)}) custom-call(bf16[2,1024,512]{2,1,0:T(8,128)(2,1)} %get-tuple-element.15.high, bf16[2,1024,512]{2,1,0:T(8,128)(2,1)} %get-tuple-element.16.low, f32[2,8,32,128]{3,2,1,0:T(8,128)} %bitcast.13), custom_call_target="tpu_custom_call" | custom-call | tf_op jit(solution)/shard_map/right/pallas_call | solution.py:100
  47.3 12.2 %all_to_all.27.raw = f32[32,8,128]{2,1,0:T(8,128)} all-to-all(f32[32,8,128]{2,1,0:T(8,128)} %bitcast.18), channel_id=1, replica_groups=mesh['dp'=32,'tensor'=8] {'dp'}, dimensions={0} | all-to-all | bytes 262144 | tf_op jit(solution)/shard_map/all_to_all | solution.py:221
  59.5 1.6 %mix.1 = f32[8,24,128]{2,1,0:T(8,128)} custom-call(f32[32,8,128]{2,1,0:T(8,128)} %all_to_all.27.raw, f32[2,8,128]{2,1,0:T(8,128)} %get-tuple-element.19.gram), custom_call_target="tpu_custom_call" | custom-call | tf_op jit(solution)/shard_map/mix/pallas_call | solution.py:123
  61.1 15.7 %all_to_all.28.x = f32[8,24,128]{2,1,0:T(8,128)} all-to-all(f32[8,24,128]{2,1,0:T(8,128)} %mix.1), channel_id=1, replica_groups=mesh['dp'=32,'tensor'=8] {'tensor'}, dimensions={0} | all-to-all | bytes 196608 | tf_op jit(solution)/shard_map/all_to_all | solution.py:221
  76.8 1.6 %unmix.1 = (f32[32,8,128]{2,1,0:T(8,128)}, f32[2,8,128]{2,1,0:T(8,128)}) custom-call(f32[8,24,128]{2,1,0:T(8,128)} %all_to_all.28.x), custom_call_target="tpu_custom_call" | custom-call | tf_op jit(solution)/shard_map/unmix/pallas_call | solution.py:133
  78.4 5.5 %all-to-all-start.4 = ((f32[32,8,128]{2,1,0:T(8,128)}), f32[32,8,128]{2,1,0:T(8,128)S(1)}, u32[]{:S(2)}, u32[]{:S(2)}) async-start(f32[32,8,128]{2,1,0:T(8,128)} %get-tuple-element.23), calls=%async_computation.4 | async-start | bytes 262144 | tf_op jit(solution)/shard_map/all_to_all | solution.py:221
  83.9 5.1 %orthonormal.1 = (f32[2,32,32]{2,1,0:T(8,128)}, bf16[2,1024,128]{2,1,0:T(8,128)(2,1)}) custom-call(f32[2,8,128]{2,1,0:T(8,128)} %get-tuple-element.20.gram, f32[2,8,32,128]{3,2,1,0:T(8,128)} %bitcast.14), custom_call_target="tpu_custom_call" | custom-call | flops 400000000 | bytes 1000000 | tf_op jit(solution)/shard_map/orthonormal/pallas_call | solution.py:170
  89.0 2.7 %all-to-all-done.4 = f32[32,8,128]{2,1,0:T(8,128)S(1)} async-done(((f32[32,8,128]{2,1,0:T(8,128)}), f32[32,8,128]{2,1,0:T(8,128)S(1)}, u32[]{:S(2)}, u32[]{:S(2)}) %all-to-all-start.4) | async-done | bytes 131104 | tf_op jit(solution)/shard_map/all_to_all | solution.py:221
  91.7 0.0 copy-start
  91.7 0.6 copy-done
  92.4 8.1 %last.1 = (bf16[2,1024,512]{2,1,0:T(8,128)(2,1)}, f32[2,1024,512]{2,1,0:T(8,128)}, f32[2,32,512]{2,1,0:T(8,128)}) custom-call(bf16[2,1024,512]{2,1,0:T(8,128)(2,1)} %get-tuple-element.15.high, bf16[2,1024,512]{2,1,0:T(8,128)(2,1)} %get-tuple-element.16.low, bf16[2,1024,128]{2,1,0:T(8,128)(2,1)} %get-tuple-element.21.p_hat, ...), custom_call_target="tpu_custom_call" | custom-call | tf_op jit(solution)/shard_map/last/pallas_call | solution.py:199
Async XLA Ops:
  78.4 13.3 %all-to-all-start.4 = ((f32[32,8,128]{2,1,0:T(8,128)}), f32[32,8,128]{2,1,0:T(8,128)S(1)}, u32[]{:S(2)}, u32[]{:S(2)}) async-start(f32[32,8,128]{2,1,0:T(8,128)} %get-tuple-element.23), calls=%async_computation.4 | async-start | bytes 262144 | tf_op jit(solution)/shard_map/all_to_all | solution.py:221
  91.7 0.7 copy-start

commit v2 on v0

v2 whole, which is shorter than its diff:
```python
import jax
import jax.numpy as jnp
from jax import lax
from jax.experimental import pallas as pl
from jax.experimental.pallas import tpu as pltpu
from jax.sharding import PartitionSpec as P

highest = lax.Precision.HIGHEST
f32, bf16 = jnp.float32, jnp.bfloat16
block_rows = 512
ahead = 3


def halves(x):
    high = x.astype(bf16)
    return high, (x - high.astype(f32)).astype(bf16)


def thirds(x):
    high = x.astype(bf16)
    rest = x - high.astype(f32)
    return high, *halves(rest)


def dot(a, b, contract, precision=None):
    return lax.dot_general(a, b, (contract, ((), ())), precision=precision, preferred_element_type=f32)


def split_dot(small, high, low, contract):
    one, two, three = small
    rows = one.shape[0]
    by_high = dot(jnp.concatenate([one, two, three], 0), high, contract)
    by_low = dot(jnp.concatenate([one, two], 0), low, contract)
    small_terms = by_high[rows : 2 * rows] + by_low[:rows]
    tiny_terms = by_high[2 * rows :] + by_low[rows:]
    return by_high[:rows] + (small_terms + tiny_terms)


def in_vmem(x):
    return pltpu.with_memory_space_constraint(x, pltpu.VMEM)


whole = pl.BlockSpec(memory_space=pltpu.VMEM)
params = pltpu.CompilerParams(vmem_limit_bytes=16 * 1024 * 1024)


def in_hbm(x):
    return pltpu.with_memory_space_constraint(x, pltpu.HBM)


def left_kernel(grads, errors, q_t, terms, part, grads_here, errors_here, q_here, q_sem, grads_sem, errors_sem):
    layers, _, rows, _ = terms.shape
    pieces = [(l, b) for l in range(layers) for b in range(rows // block_rows)]

    def fetch(n):
        l, b = pieces[n]
        at = pl.ds(b * block_rows, block_rows)
        return (
            pltpu.make_async_copy(grads.at[l, at], grads_here.at[l, at], grads_sem.at[n]),
            pltpu.make_async_copy(errors.at[l, at], errors_here.at[l, at], errors_sem.at[n]),
        )

    q_copy = pltpu.make_async_copy(q_t, q_here, q_sem)
    q_copy.start()
    for n in range(ahead):
        for copy in fetch(n):
            copy.start()
    q_copy.wait()
    for n, (l, b) in enumerate(pieces):
        for copy in fetch(n):
            copy.wait()
        if n + ahead < len(pieces):
            for copy in fetch(n + ahead):
                copy.start()
        at = pl.ds(b * block_rows, block_rows)
        merged = grads_here[l, at].astype(f32) + errors_here[l, at]
        merged_high, merged_low = halves(merged)
        terms[l, 0, at] = merged_high
        terms[l, 1, at] = merged_low
        term = split_dot(thirds(q_here[l]), merged_high, merged_low, ((1,), (1,)))
        for lane in range(block_rows // 128):
            part[l, b * (block_rows // 128) + lane] = term[:, lane * 128 : (lane + 1) * 128]


def left(grads, errors, q_t):
    layers, rows, cols = grads.shape
    rank = q_t.shape[1]
    pieces = layers * rows // block_rows
    return pl.pallas_call(
        left_kernel,
        in_specs=[pl.BlockSpec(memory_space=pltpu.HBM)] * 3,
        out_specs=[whole] * 2,
        out_shape=[
            pltpu.VMEM((layers, 2, rows, cols), bf16),
            pltpu.VMEM((layers, rows // 128, rank, 128), f32),
        ],
        scratch_shapes=[
            pltpu.VMEM(grads.shape, bf16),
            pltpu.VMEM(grads.shape, f32),
            pltpu.VMEM(q_t.shape, f32),
            pltpu.SemaphoreType.DMA,
            pltpu.SemaphoreType.DMA((pieces,)),
            pltpu.SemaphoreType.DMA((pieces,)),
        ],
        compiler_params=params,
        name="left",
    )(in_hbm(grads), in_hbm(errors), in_hbm(q_t))


def spread(x, scale):
    def kernel(x, out):
        total = jnp.sum(x[...], axis=0) * scale
        out[...] = jnp.broadcast_to(total[None], out.shape)

    return pl.pallas_call(
        kernel,
        in_specs=[whole],
        out_specs=whole,
        out_shape=pltpu.VMEM(x.shape, f32),
        compiler_params=params,
        name="spread",
    )(in_vmem(x))


def right_kernel(terms, p_t, raw, gram, p_terms):
    layers, tiles, rank, _ = p_t.shape
    for l in range(layers):
        factor = jnp.concatenate([p_t[l, at] for at in range(tiles)], 1)
        small = thirds(factor)
        term = split_dot(small, terms[l, 0], terms[l, 1], ((1,), (0,)))
        for at in range(raw.shape[1]):
            raw[l, at] = term[:, at * 128 : (at + 1) * 128]
        square = dot(factor, factor, ((1,), (1,)), highest)
        gram[l] = jnp.concatenate([square[at : at + 8] for at in range(0, rank, 8)], 1)
        stack = jnp.concatenate([small[0], small[1], small[0], jnp.zeros_like(small[0])], 0)
        p_terms[l] = stack.T


def right(terms, p_t):
    layers, _, rows, cols = terms.shape
    rank = p_t.shape[2]
    return pl.pallas_call(
        right_kernel,
        in_specs=[whole] * 2,
        out_specs=[whole] * 3,
        out_shape=[
            pltpu.VMEM((layers, cols // 128, rank, 128), f32),
            pltpu.VMEM((layers, 8, 128), f32),
            pltpu.VMEM((layers, rows, 4 * rank), bf16),
        ],
        compiler_params=params,
        name="right",
    )(in_vmem(terms), in_vmem(p_t))


def mix(raw, gram, copies):
    def kernel(raw, gram, out):
        total = jnp.sum(raw[...], axis=0)
        both = jnp.concatenate([total, gram[0], gram[1]], 0)
        out[...] = jnp.broadcast_to(both[None], out.shape)

    return pl.pallas_call(
        kernel,
        in_specs=[whole] * 2,
        out_specs=whole,
        out_shape=pltpu.VMEM((copies, raw.shape[1] + 16, 128), f32),
        compiler_params=params,
        name="mix",
    )(in_vmem(raw), in_vmem(gram))


def lower_inverses(packed, rank):
    groups = rank // 8
    row = lax.broadcasted_iota(jnp.int32, (8, 128), 0)
    lane = lax.broadcasted_iota(jnp.int32, (8, 128), 1)
    first = (lane // rank) % 2 == 0
    tiles = []
    for g in range(groups):
        squares = [tile[:, g * rank : (g + 1) * rank] for tile in packed]
        unit = (lane % rank == row + 8 * g).astype(f32)
        tiles.append(jnp.concatenate(squares + [unit[:, 2 * rank :]], 1))
    pivots = [jnp.ones((8, 128), f32)] * groups
    for start in range(0, rank, 16):
        columns = {}
        for k in range(start, start + 16):
            for g in range(start // 8, groups):
                columns[k, g] = jnp.where(first, tiles[g][:, k : k + 1], tiles[g][:, rank + k : rank + k + 1])
        for k in range(start, start + 16):
            at, s = divmod(k, 8)
            pivot = columns[k, at][s : s + 1]
            pivots[at] = jnp.where(row == s, pivot, pivots[at])
            over = 1.0 / pivot
            pivot_row = tiles[at][s : s + 1] * over
            entries = {j: columns[j, at][s : s + 1] * over for j in range(k + 1, start + 16)}
            for g in range(at, groups):
                column = columns[k, g]
                if g == at:
                    column = jnp.where(row > s, column, 0.0)
                tiles[g] = tiles[g] - column * pivot_row
                for j, entry in entries.items():
                    columns[j, g] = columns[j, g] - column * entry
    both = jnp.concatenate([tile / jnp.sqrt(pivot) for tile, pivot in zip(tiles, pivots)], 0)
    return [both[:, (2 + l) * rank : (3 + l) * rank] for l in range(2)]


def unmix(x, copies, rank, scale):
    def kernel(x, piece, inverse):
        total = jnp.sum(x[...], axis=0)
        piece[...] = jnp.broadcast_to(total[None, :8] * scale, piece.shape)
        inverse[0], inverse[1] = lower_inverses([total[8:16], total[16:24]], rank)

    return pl.pallas_call(
        kernel,
        in_specs=[whole],
        out_specs=[whole] * 2,
        out_shape=[pltpu.VMEM((copies, 8, 128), f32), pltpu.VMEM((2, rank, rank), f32)],
        compiler_params=params,
        name="unmix",
    )(in_vmem(x))


def last_kernel(
    terms, p_terms, inverse, raw, decompressed, new_errors, q_new,
    decompressed_here, errors_here, q_here, decompressed_sem, errors_sem, q_sem,
):
    layers, _, rows, _ = terms.shape
    copies = []

    def send(source, target, sem):
        copy = pltpu.make_async_copy(source, target, sem)
        copy.start()
        copies.append(copy)

    for l in range(layers):
        sums = jnp.concatenate([raw[l, at] for at in range(raw.shape[1])], 1)
        q = dot(inverse[l], sums, ((1,), (0,)), highest)
        q_here[l] = q
        send(q_here.at[l], q_new.at[l], q_sem.at[l])
        right_high, right_low = halves(dot(inverse[l], q, ((0,), (0,)), highest))
        stack = jnp.concatenate([right_high, right_high, right_low, jnp.zeros_like(right_high)], 0)
        for b in range(rows // block_rows):
            at = pl.ds(b * block_rows, block_rows)
            n = l * (rows // block_rows) + b
            approx = dot(p_terms[l, at], stack, ((1,), (0,)))
            decompressed_here[l, at] = approx.astype(bf16)
            errors_here[l, at] = (terms[l, 0, at].astype(f32) + terms[l, 1, at].astype(f32)) - approx
            send(decompressed_here.at[l, at], decompressed.at[l, at], decompressed_sem.at[n])
            send(errors_here.at[l, at], new_errors.at[l, at], errors_sem.at[n])
    for copy in copies:
        copy.wait()


def last(terms, p_terms, inverse, raw):
    layers, _, rows, cols = terms.shape
    shape = (layers, rows, cols)
    rank = inverse.shape[1]
    pieces = layers * rows // block_rows
    return pl.pallas_call(
        last_kernel,
        in_specs=[whole] * 4,
        out_specs=[pl.BlockSpec(memory_space=pltpu.HBM)] * 3,
        out_shape=[
            pltpu.HBM(shape, bf16),
            pltpu.HBM(shape, f32),
            pltpu.HBM((layers, rank, cols), f32),
        ],
        scratch_shapes=[
            pltpu.VMEM(shape, bf16),
            pltpu.VMEM(shape, f32),
            pltpu.VMEM((layers, rank, cols), f32),
            pltpu.SemaphoreType.DMA((pieces,)),
            pltpu.SemaphoreType.DMA((pieces,)),
            pltpu.SemaphoreType.DMA((layers,)),
        ],
        compiler_params=params,
        name="last",
    )(in_vmem(terms), in_vmem(p_terms), in_vmem(inverse), in_vmem(raw))


def exchange(x, axis):
    return lax.all_to_all(x, axis, 0, 0, tiled=True)


def on_device(grads, errors, q_prev):
    replicas, slabs = lax.axis_size("dp"), lax.axis_size("tensor")
    terms, part = left(grads[:, 0], errors[:, 0], jnp.swapaxes(q_prev, 1, 2))
    tiles_shape = part.shape
    part = exchange(part.reshape(replicas, -1, 128), "dp")
    p_t = exchange(spread(part, 1.0 / replicas), "dp").reshape(tiles_shape)
    raw, gram, p_terms = right(terms, p_t)
    raw_shape = raw.shape
    raw = exchange(raw.reshape(replicas, -1, 128), "dp")
    both = exchange(mix(raw, gram, slabs), "tensor")
    raw, inverse = unmix(both, replicas, p_t.shape[2], 1.0 / replicas)
    raw = exchange(raw, "dp").reshape(raw_shape)
    decompressed, new_errors, q_new = last(terms, p_terms, inverse, raw)
    return decompressed, new_errors[:, None], jnp.swapaxes(q_new, 1, 2)


def solution(mesh):
    placed = (P(None, "dp", "tensor", None), P(None, "dp", "tensor", None), P())
    return jax.shard_map(
        on_device,
        mesh=mesh,
        in_specs=placed,
        out_specs=(P(None, "tensor", None), P(None, "dp", "tensor", None), P()),
        check_vma=False,
    )
```

time: 434 us -> 79.5 us (0.18)
  waiting for transfers between devices: 360 us -> 0 us
  blocking collectives: 23 us -> 69.3 us
  matrix products: 23.2 us -> 0 us
  between operations: 14.1 us -> 0.65 us
  other arithmetic: 11.9 us -> 0 us
  Pallas kernels: 0 us -> 9.32 us
    psum x2 -> x0, waiting for transfers between devices: 360 us -> none  [the longest x1 245 us: on_device(): right = lax.psum(right_term, ('dp', 'tensor')) / replicas]
    all_to_all x0 -> x5, blocking collectives: none -> 69.3 us  [exchange(): return lax.all_to_all(x, axis, 0, 0, tiled=True)]
    psum x1 -> x0, blocking collectives: 23 us -> none  [on_device(): p_hat = by_gram(factor, lambda gram: lax.psum(gram, 'tensor'))]
    dot_general x4 -> x0, matrix products: 21.9 us -> none  [the longest x1 7.59 us: on_device(): left_term = jnp.einsum('lrc,lck->lrk', merged, q_prev, precision=highest)]
    another operation x7 -> x0, other arithmetic: 11 us -> none  [the longest x4 6.03 us: by_gram(): lower = jnp.linalg.cholesky(gram)]
    pallas_call x0 -> x6, Pallas kernels: none -> 9.32 us  [the longest x1 3.92 us: left(): pl.pallas_call(left_kernel, in_specs=[pl.BlockSpec(memory_space=pltpu.HBM...]
  transfers between devices with their start and end apart: 2 -> 0, of which waited for: 2 -> 0; matrix products, arithmetic and copies ran while one was open for 0% -> 0% of each run, Pallas kernels for 0% -> 0%
where the time goes in v2:
time: 79.5 us; the launch traced here: 79.2 us
  blocking collectives  69.3 us (87%)
  Pallas kernels  9.32 us (12%)
    all_to_all x5, blocking collectives, exchange(): return lax.all_to_all(x, axis, 0, 0, tiled=True)  69.3 us
    pallas_call x1, Pallas kernels, left(): pl.pallas_call(left_kernel, in_specs=[pl.BlockSpec(memory_space=pltpu.HBM...  3.92 us
    pallas_call x1, Pallas kernels, last(): pl.pallas_call(last_kernel, in_specs=[whole] * 4, out_specs=[pl.BlockSpec...  3.5 us

profile of v2, /device:TPU:1, one launch (start us, length us, event | category | flops | bytes accessed | tf_op | source)
XLA Modules:
  0.0 79.2 jit_solution(5274868877422796216)
XLA Ops:
  0.6 3.9 %left.1 = (bf16[2,2,1024,512]{3,2,1,0:T(8,128)(2,1)S(1)}, f32[2,8,32,128]{3,2,1,0:T(8,128)S(1)}) custom-call(bf16[2,1024,512]{2,1,0:T(8,128)(2,1)} %bitcast.16, f32[2,1024,512]{2,1,0:T(8,128)} %bitcast.15, f32[2,32,512]{2,1,0:T(8,128)} %bitcast.17), custom_call_target="tpu_custom_call" | custom-call | tf_op jit(solution)/shard_map/left/pallas_call | solution.py:89
  4.6 17.4 %all_to_all.25.x = f32[32,16,128]{2,1,0:T(8,128)S(1)} all-to-all(f32[32,16,128]{2,1,0:T(8,128)S(1)} %bitcast.13), channel_id=1, replica_groups=mesh['dp'=32,'tensor'=8] {'dp'}, dimensions={0} | all-to-all | bytes 524288 | tf_op jit(solution)/shard_map/all_to_all | solution.py:281
  21.9 0.1 spread.1
  22.0 12.5 %all_to_all.26 = f32[32,16,128]{2,1,0:T(8,128)S(1)} all-to-all(f32[32,16,128]{2,1,0:T(8,128)S(1)} %spread.1), channel_id=1, replica_groups=mesh['dp'=32,'tensor'=8] {'dp'}, dimensions={0} | all-to-all | bytes 524288 | tf_op jit(solution)/shard_map/all_to_all | solution.py:281
  34.4 1.1 %right.1 = (f32[2,4,32,128]{3,2,1,0:T(8,128)S(1)}, f32[2,8,128]{2,1,0:T(8,128)S(1)}, bf16[2,1024,128]{2,1,0:T(8,128)(2,1)S(1)}) custom-call(bf16[2,2,1024,512]{3,2,1,0:T(8,128)(2,1)S(1)} %get-tuple-element.13.terms, f32[2,8,32,128]{3,2,1,0:T(8,128)S(1)} %bitcast.11), custom_call_target="tpu_custom_call" | custom-call | tf_op jit(solution)/shard_map/right/pallas_call | solution.py:142
  35.5 11.2 %all_to_all.27.raw = f32[32,8,128]{2,1,0:T(8,128)S(1)} all-to-all(f32[32,8,128]{2,1,0:T(8,128)S(1)} %bitcast.14), channel_id=1, replica_groups=mesh['dp'=32,'tensor'=8] {'dp'}, dimensions={0} | all-to-all | bytes 262144 | tf_op jit(solution)/shard_map/all_to_all | solution.py:281
  46.7 15.4 %all_to_all.28.x = f32[8,24,128]{2,1,0:T(8,128)S(1)} all-to-all(f32[8,24,128]{2,1,0:T(8,128)S(1)} %mix.1), channel_id=1, replica_groups=mesh['dp'=32,'tensor'=8] {'tensor'}, dimensions={0} | all-to-all | bytes 196608 | tf_op jit(solution)/shard_map/all_to_all | solution.py:281
  62.2 0.7 unmix.1
  62.9 12.8 %all_to_all.29 = f32[32,8,128]{2,1,0:T(8,128)S(1)} all-to-all(f32[32,8,128]{2,1,0:T(8,128)S(1)} %get-tuple-element.19), channel_id=1, replica_groups=mesh['dp'=32,'tensor'=8] {'dp'}, dimensions={0} | all-to-all | bytes 262144 | tf_op jit(solution)/shard_map/all_to_all | solution.py:281
  75.7 3.5 %last.1 = (bf16[2,1024,512]{2,1,0:T(8,128)(2,1)}, f32[2,1024,512]{2,1,0:T(8,128)}, f32[2,32,512]{2,1,0:T(8,128)}) custom-call(bf16[2,2,1024,512]{3,2,1,0:T(8,128)(2,1)S(1)} %get-tuple-element.13.terms, bf16[2,1024,128]{2,1,0:T(8,128)(2,1)S(1)} %get-tuple-element.15.p_terms, f32[2,32,32]{2,1,0:T(8,128)S(1)} %get-tuple-element.18.inverse, ...), custom_call_target="tpu_custom_call" | custom-call | tf_op jit(solution)/shard_map/last/pallas_call | solution.py:258
  (1 shorter events, 0.0 us)

commit v3 on v2

--- a/solution.py
+++ b/solution.py
@@ -36,6 +36,10 @@
     return by_high[:rows] + (small_terms + tiny_terms)
 
 
+def this_core():
+    return lax.axis_index("dp") % 2
+
+
 def in_vmem(x):
     return pltpu.with_memory_space_constraint(x, pltpu.VMEM)
 
@@ -48,9 +52,10 @@
     return pltpu.with_memory_space_constraint(x, pltpu.HBM)
 
 
-def left_kernel(grads, errors, q_t, terms, part, grads_here, errors_here, q_here, q_sem, grads_sem, errors_sem):
+def left_kernel(grads, errors, q_t, terms, other, own, grads_here, errors_here, q_here, q_sem, grads_sem, errors_sem):
     layers, _, rows, _ = terms.shape
-    pieces = [(l, b) for l in range(layers) for b in range(rows // block_rows)]
+    core = this_core()
+    pieces = [(l, b) for l in (1 - core, core) for b in range(rows // block_rows)]
 
     def fetch(n):
         l, b = pieces[n]
@@ -78,8 +83,9 @@
         terms[l, 0, at] = merged_high
         terms[l, 1, at] = merged_low
         term = split_dot(thirds(q_here[l]), merged_high, merged_low, ((1,), (1,)))
+        part = other if n < len(pieces) // 2 else own
         for lane in range(block_rows // 128):
-            part[l, b * (block_rows // 128) + lane] = term[:, lane * 128 : (lane + 1) * 128]
+            part[b * (block_rows // 128) + lane] = term[:, lane * 128 : (lane + 1) * 128]
 
 
 def left(grads, errors, q_t):
@@ -89,10 +95,11 @@
     return pl.pallas_call(
         left_kernel,
         in_specs=[pl.BlockSpec(memory_space=pltpu.HBM)] * 3,
-        out_specs=[whole] * 2,
+        out_specs=[whole] * 3,
         out_shape=[
             pltpu.VMEM((layers, 2, rows, cols), bf16),
-            pltpu.VMEM((layers, rows // 128, rank, 128), f32),
+            pltpu.VMEM((rows // 128, rank, 128), f32),
+            pltpu.VMEM((rows // 128, rank, 128), f32),
         ],
         scratch_shapes=[
             pltpu.VMEM(grads.shape, bf16),
@@ -107,25 +114,26 @@
     )(in_hbm(grads), in_hbm(errors), in_hbm(q_t))
 
 
-def spread(x, scale):
-    def kernel(x, out):
-        total = jnp.sum(x[...], axis=0) * scale
-        out[...] = jnp.broadcast_to(total[None], out.shape)
+def add(x, y, scale=1.0):
+    def kernel(x, y, out):
+        out[...] = (x[...] + y[...]) * scale
 
     return pl.pallas_call(
         kernel,
-        in_specs=[whole],
+        in_specs=[whole] * 2,
         out_specs=whole,
         out_shape=pltpu.VMEM(x.shape, f32),
         compiler_params=params,
-        name="spread",
-    )(in_vmem(x))
-
-
-def right_kernel(terms, p_t, raw, gram, p_terms):
-    layers, tiles, rank, _ = p_t.shape
+        name="add",
+    )(in_vmem(x), in_vmem(y))
+
+
+def right_kernel(terms, p_own, p_other, raw, gram, p_terms):
+    layers = terms.shape[0]
+    tiles, rank, _ = p_own.shape
+    core = this_core()
     for l in range(layers):
-        factor = jnp.concatenate([p_t[l, at] for at in range(tiles)], 1)
+        factor = jnp.concatenate([jnp.where(core == l, p_own[at], p_other[at]) for at in range(tiles)], 1)
         small = thirds(factor)
         term = split_dot(small, terms[l, 0], terms[l, 1], ((1,), (0,)))
         for at in range(raw.shape[1]):
@@ -136,12 +144,12 @@
         p_terms[l] = stack.T
 
 
-def right(terms, p_t):
+def right(terms, p_own, p_other):
     layers, _, rows, cols = terms.shape
-    rank = p_t.shape[2]
+    rank = p_own.shape[1]
     return pl.pallas_call(
         right_kernel,
-        in_specs=[whole] * 2,
+        in_specs=[whole] * 3,
         out_specs=[whole] * 3,
         out_shape=[
             pltpu.VMEM((layers, cols // 128, rank, 128), f32),
@@ -150,7 +158,7 @@
         ],
         compiler_params=params,
         name="right",
-    )(in_vmem(terms), in_vmem(p_t))
+    )(in_vmem(terms), in_vmem(p_own), in_vmem(p_other))
 
 
 def mix(raw, gram, copies):
@@ -281,17 +289,35 @@
     return lax.all_to_all(x, axis, 0, 0, tiled=True)
 
 
+def swap(x, partner):
+    replicas = lax.axis_size("dp")
+    pairs = []
+    for device in range(replicas):
+        px, py, core = partner(device // 8, device // 2 % 4, device % 2)
+        pairs.append((device, (px * 4 + py) * 2 + core))
+    return lax.ppermute(x, "dp", pairs)
+
+
+def sum_left(other, own, scale):
+    total = add(own, swap(other, lambda x, y, core: (x, y, 1 - core)))
+    for at, (first, second) in enumerate([((1, 0), (0, 1)), ((3, 0), (0, 3)), ((0, 1), (1, 0)), ((0, 3), (3, 0))]):
+
+        def partner(x, y, core):
+            dx, dy = (first, second)[core]
+            return x ^ dx, y ^ dy, core
+
+        total = add(total, swap(total, partner), scale if at == 3 else 1.0)
+    return total, swap(total, lambda x, y, core: (x, y, 1 - core))
+
+
 def on_device(grads, errors, q_prev):
-    replicas, slabs = lax.axis_size("dp"), lax.axis_size("tensor")
-    terms, part = left(grads[:, 0], errors[:, 0], jnp.swapaxes(q_prev, 1, 2))
-    tiles_shape = part.shape
-    part = exchange(part.reshape(replicas, -1, 128), "dp")
-    p_t = exchange(spread(part, 1.0 / replicas), "dp").reshape(tiles_shape)
-    raw, gram, p_terms = right(terms, p_t)
+    replicas, slabs, rank = lax.axis_size("dp"), lax.axis_size("tensor"), q_prev.shape[2]
+    terms, other, own = left(grads[:, 0], errors[:, 0], jnp.swapaxes(q_prev, 1, 2))
+    raw, gram, p_terms = right(terms, *sum_left(other, own, 1.0 / replicas))
     raw_shape = raw.shape
     raw = exchange(raw.reshape(replicas, -1, 128), "dp")
     both = exchange(mix(raw, gram, slabs), "tensor")
-    raw, inverse = unmix(both, replicas, p_t.shape[2], 1.0 / replicas)
+    raw, inverse = unmix(both, replicas, rank, 1.0 / replicas)
     raw = exchange(raw, "dp").reshape(raw_shape)
     decompressed, new_errors, q_new = last(terms, p_terms, inverse, raw)
     return decompressed, new_errors[:, None], jnp.swapaxes(q_new, 1, 2)

time: 79.5 us -> 79.4 us (level)
  blocking collectives: 69.3 us -> 41 us
  waiting for transfers between devices: 0 us -> 18.1 us
  starting transfers between devices: 0 us -> 10.2 us
    all_to_all x5 -> x3, blocking collectives: 69.3 us -> 41 us  [exchange(): return lax.all_to_all(x, axis, 0, 0, tiled=True)]
    ppermute x0 -> x6, waiting for transfers between devices: none -> 18.1 us  [swap(): return lax.ppermute(x, 'dp', pairs)]
    ppermute x0 -> x6, starting transfers between devices: none -> 10.2 us  [swap(): return lax.ppermute(x, 'dp', pairs)]
  transfers between devices with their start and end apart: 0 -> 6, of which waited for: 0 -> 6; matrix products, arithmetic and copies ran while one was open for 0% -> 0% of each run, Pallas kernels for 0% -> 0%
where the time goes in v3:
time: 79.4 us; the launch traced here: 79.2 us
  blocking collectives  41 us (52%)
  waiting for transfers between devices  18.1 us (23%)
  starting transfers between devices  10.2 us (13%)
  Pallas kernels  9.07 us (11%)
    all_to_all x3, blocking collectives, exchange(): return lax.all_to_all(x, axis, 0, 0, tiled=True)  41 us
    ppermute x6, waiting for transfers between devices, swap(): return lax.ppermute(x, 'dp', pairs)  18.1 us
    ppermute x6, starting transfers between devices, swap(): return lax.ppermute(x, 'dp', pairs)  10.2 us
    pallas_call x1, Pallas kernels, left(): pl.pallas_call(left_kernel, in_specs=[pl.BlockSpec(memory_space=pltpu.HBM...  3.65 us
    pallas_call x1, Pallas kernels, last(): pl.pallas_call(last_kernel, in_specs=[whole] * 4, out_specs=[pl.BlockSpec...  3.5 us
  transfers between devices with their start and end apart: 6, of which 6 were waited for; matrix products, arithmetic and copies ran while one was open for 0% of the time, Pallas kernels for 0%

profile of v3, /device:TPU:1, one launch (start us, length us, event | category | flops | bytes accessed | tf_op | source)
XLA Modules:
  0.0 79.2 jit_solution(5946688568405392650)
XLA Ops:
  0.6 3.6 %left.1 = (bf16[2,2,1024,512]{3,2,1,0:T(8,128)(2,1)S(1)}, f32[8,32,128]{2,1,0:T(8,128)S(1)}, f32[8,32,128]{2,1,0:T(8,128)S(1)}) custom-call(bf16[2,1024,512]{2,1,0:T(8,128)(2,1)} %bitcast.12, f32[2,1024,512]{2,1,0:T(8,128)} %bitcast.11, f32[2,32,512]{2,1,0:T(8,128)} %bitcast.13), custom_call_target="tpu_custom_call" | custom-call | tf_op jit(solution)/shard_map/left/pallas_call | solution.py:95
  4.3 3.3 %collective-permute-start = (f32[8,32,128]{2,1,0:T(8,128)S(1)}, f32[8,32,128]{2,1,0:T(8,128)S(1)}, u32[]{:S(2)}, u32[]{:S(2)}) collective-permute-start(f32[8,32,128]{2,1,0:T(8,128)S(1)} %get-tuple-element.16), channel_id=1, source_target_pairs={{0,8},{8,0},{16,24},{24,16},{32,40},{40,32},{48,56},{56,48},{64,72... | collective-permute-start | bytes 393224 | tf_op jit(solution)/shard_map/ppermute | solution.py:298
  7.6 1.0 %collective-permute-done.y = f32[8,32,128]{2,1,0:T(8,128)S(1)} collective-permute-done((f32[8,32,128]{2,1,0:T(8,128)S(1)}, f32[8,32,128]{2,1,0:T(8,128)S(1)}, u32[]{:S(2)}, u32[]{:S(2)}) %collective-permute-start) | collective-permute-done | bytes 131104 | tf_op jit(solution)/shard_map/ppermute | solution.py:298
  8.6 0.1 collective-permute-start.1
  8.7 4.1 %collective-permute-done.1.y = f32[8,32,128]{2,1,0:T(8,128)S(1)} collective-permute-done((f32[8,32,128]{2,1,0:T(8,128)S(1)}, f32[8,32,128]{2,1,0:T(8,128)S(1)}, u32[]{:S(2)}, u32[]{:S(2)}) %collective-permute-start.1) | collective-permute-done | bytes 131104 | tf_op jit(solution)/shard_map/ppermute | solution.py:298
  12.8 1.1 %collective-permute-start.2 = (f32[8,32,128]{2,1,0:T(8,128)S(1)}, f32[8,32,128]{2,1,0:T(8,128)S(1)}, u32[]{:S(2)}, u32[]{:S(2)}) collective-permute-start(f32[8,32,128]{2,1,0:T(8,128)S(1)} %add.6.x), channel_id=1, source_target_pairs={{0,192},{8,56},{16,208},{24,40},{32,224},{40,24},{48,240},{56,8},{... | collective-permute-start | bytes 393224 | tf_op jit(solution)/shard_map/ppermute | solution.py:298
  13.9 4.0 %collective-permute-done.2.y = f32[8,32,128]{2,1,0:T(8,128)S(1)} collective-permute-done((f32[8,32,128]{2,1,0:T(8,128)S(1)}, f32[8,32,128]{2,1,0:T(8,128)S(1)}, u32[]{:S(2)}, u32[]{:S(2)}) %collective-permute-start.2) | collective-permute-done | bytes 131104 | tf_op jit(solution)/shard_map/ppermute | solution.py:298
  18.0 0.1 collective-permute-start.3
  18.1 3.8 %collective-permute-done.3.y = f32[8,32,128]{2,1,0:T(8,128)S(1)} collective-permute-done((f32[8,32,128]{2,1,0:T(8,128)S(1)}, f32[8,32,128]{2,1,0:T(8,128)S(1)}, u32[]{:S(2)}, u32[]{:S(2)}) %collective-permute-start.3) | collective-permute-done | bytes 131104 | tf_op jit(solution)/shard_map/ppermute | solution.py:298
  21.9 0.9 %collective-permute-start.4 = (f32[8,32,128]{2,1,0:T(8,128)S(1)}, f32[8,32,128]{2,1,0:T(8,128)S(1)}, u32[]{:S(2)}, u32[]{:S(2)}) collective-permute-start(f32[8,32,128]{2,1,0:T(8,128)S(1)} %add.8.x), channel_id=1, source_target_pairs={{0,48},{8,200},{16,32},{24,216},{32,16},{40,232},{48,0},{56,248},{... | collective-permute-start | bytes 393224 | tf_op jit(solution)/shard_map/ppermute | solution.py:298
  22.8 4.2 %collective-permute-done.4.y = f32[8,32,128]{2,1,0:T(8,128)S(1)} collective-permute-done((f32[8,32,128]{2,1,0:T(8,128)S(1)}, f32[8,32,128]{2,1,0:T(8,128)S(1)}, u32[]{:S(2)}, u32[]{:S(2)}) %collective-permute-start.4) | collective-permute-done | bytes 131104 | tf_op jit(solution)/shard_map/ppermute | solution.py:298
  27.0 4.8 %collective-permute-start.5 = (f32[8,32,128]{2,1,0:T(8,128)S(1)}, f32[8,32,128]{2,1,0:T(8,128)S(1)}, u32[]{:S(2)}, u32[]{:S(2)}) collective-permute-start(f32[8,32,128]{2,1,0:T(8,128)S(1)} %add.9.p_own), channel_id=1, source_target_pairs={{0,8},{8,0},{16,24},{24,16},{32,40},{40,32},{48,56},{56,48},{64,72... | collective-permute-start | bytes 393224 | tf_op jit(solution)/shard_map/ppermute | solution.py:298
  31.8 1.0 %collective-permute-done.5.p_other = f32[8,32,128]{2,1,0:T(8,128)S(1)} collective-permute-done((f32[8,32,128]{2,1,0:T(8,128)S(1)}, f32[8,32,128]{2,1,0:T(8,128)S(1)}, u32[]{:S(2)}, u32[]{:S(2)}) %collective-permute-start.5) | collective-permute-done | bytes 131104 | tf_op jit(solution)/shard_map/ppermute | solution.py:298
  32.8 1.1 %right.1 = (f32[2,4,32,128]{3,2,1,0:T(8,128)S(1)}, f32[2,8,128]{2,1,0:T(8,128)S(1)}, bf16[2,1024,128]{2,1,0:T(8,128)(2,1)S(1)}) custom-call(bf16[2,2,1024,512]{3,2,1,0:T(8,128)(2,1)S(1)} %get-tuple-element.14.terms, f32[8,32,128]{2,1,0:T(8,128)S(1)} %add.9.p_own, f32[8,32,128]{2,1,0:T(8,128)S(1)} %collective-permute-done.5.p_other), custom_call_target="tpu_custom_call" | custom-call | tf_op jit(solution)/shard_map/right/pallas_call | solution.py:150
  33.9 12.8 %all_to_all.15.raw = f32[32,8,128]{2,1,0:T(8,128)S(1)} all-to-all(f32[32,8,128]{2,1,0:T(8,128)S(1)} %bitcast.10), channel_id=1, replica_groups=mesh['dp'=32,'tensor'=8] {'dp'}, dimensions={0} | all-to-all | bytes 262144 | tf_op jit(solution)/shard_map/all_to_all | solution.py:289
  46.7 15.4 %all_to_all.16.x = f32[8,24,128]{2,1,0:T(8,128)S(1)} all-to-all(f32[8,24,128]{2,1,0:T(8,128)S(1)} %mix.1), channel_id=1, replica_groups=mesh['dp'=32,'tensor'=8] {'tensor'}, dimensions={0} | all-to-all | bytes 196608 | tf_op jit(solution)/shard_map/all_to_all | solution.py:289
  62.1 0.7 unmix.1
  62.8 12.8 %all_to_all.17 = f32[32,8,128]{2,1,0:T(8,128)S(1)} all-to-all(f32[32,8,128]{2,1,0:T(8,128)S(1)} %get-tuple-element.21), channel_id=1, replica_groups=mesh['dp'=32,'tensor'=8] {'dp'}, dimensions={0} | all-to-all | bytes 262144 | tf_op jit(solution)/shard_map/all_to_all | solution.py:289
  75.7 3.5 %last.1 = (bf16[2,1024,512]{2,1,0:T(8,128)(2,1)}, f32[2,1024,512]{2,1,0:T(8,128)}, f32[2,32,512]{2,1,0:T(8,128)}) custom-call(bf16[2,2,1024,512]{3,2,1,0:T(8,128)(2,1)S(1)} %get-tuple-element.14.terms, bf16[2,1024,128]{2,1,0:T(8,128)(2,1)S(1)} %get-tuple-element.17.p_terms, f32[2,32,32]{2,1,0:T(8,128)S(1)} %get-tuple-element.20.inverse, ...), custom_call_target="tpu_custom_call" | custom-call | tf_op jit(solution)/shard_map/last/pallas_call | solution.py:266
  (6 shorter events, 0.1 us)
Async XLA Ops:
  4.3 4.3 %collective-permute-start = (f32[8,32,128]{2,1,0:T(8,128)S(1)}, f32[8,32,128]{2,1,0:T(8,128)S(1)}, u32[]{:S(2)}, u32[]{:S(2)}) collective-permute-start(f32[8,32,128]{2,1,0:T(8,128)S(1)} %get-tuple-element.16), channel_id=1, source_target_pairs={{0,8},{8,0},{16,24},{24,16},{32,40},{40,32},{48,56},{56,48},{64,72... | collective-permute-start | bytes 393224 | tf_op jit(solution)/shard_map/ppermute | solution.py:298
  8.6 4.2 %collective-permute-start.1 = (f32[8,32,128]{2,1,0:T(8,128)S(1)}, f32[8,32,128]{2,1,0:T(8,128)S(1)}, u32[]{:S(2)}, u32[]{:S(2)}) collective-permute-start(f32[8,32,128]{2,1,0:T(8,128)S(1)} %add.5.x), channel_id=1, source_target_pairs={{0,64},{8,24},{16,80},{24,8},{32,96},{40,56},{48,112},{56,40},{64,... | collective-permute-start | bytes 393224 | tf_op jit(solution)/shard_map/ppermute | solution.py:298
  12.8 5.1 %collective-permute-start.2 = (f32[8,32,128]{2,1,0:T(8,128)S(1)}, f32[8,32,128]{2,1,0:T(8,128)S(1)}, u32[]{:S(2)}, u32[]{:S(2)}) collective-permute-start(f32[8,32,128]{2,1,0:T(8,128)S(1)} %add.6.x), channel_id=1, source_target_pairs={{0,192},{8,56},{16,208},{24,40},{32,224},{40,24},{48,240},{56,8},{... | collective-permute-start | bytes 393224 | tf_op jit(solution)/shard_map/ppermute | solution.py:298
  18.0 3.9 %collective-permute-start.3 = (f32[8,32,128]{2,1,0:T(8,128)S(1)}, f32[8,32,128]{2,1,0:T(8,128)S(1)}, u32[]{:S(2)}, u32[]{:S(2)}) collective-permute-start(f32[8,32,128]{2,1,0:T(8,128)S(1)} %add.7.x), channel_id=1, source_target_pairs={{0,16},{8,72},{16,0},{24,88},{32,48},{40,104},{48,32},{56,120},{64... | collective-permute-start | bytes 393224 | tf_op jit(solution)/shard_map/ppermute | solution.py:298
  21.9 5.1 %collective-permute-start.4 = (f32[8,32,128]{2,1,0:T(8,128)S(1)}, f32[8,32,128]{2,1,0:T(8,128)S(1)}, u32[]{:S(2)}, u32[]{:S(2)}) collective-permute-start(f32[8,32,128]{2,1,0:T(8,128)S(1)} %add.8.x), channel_id=1, source_target_pairs={{0,48},{8,200},{16,32},{24,216},{32,16},{40,232},{48,0},{56,248},{... | collective-permute-start | bytes 393224 | tf_op jit(solution)/shard_map/ppermute | solution.py:298
  27.0 5.7 %collective-permute-start.5 = (f32[8,32,128]{2,1,0:T(8,128)S(1)}, f32[8,32,128]{2,1,0:T(8,128)S(1)}, u32[]{:S(2)}, u32[]{:S(2)}) collective-permute-start(f32[8,32,128]{2,1,0:T(8,128)S(1)} %add.9.p_own), channel_id=1, source_target_pairs={{0,8},{8,0},{16,24},{24,16},{32,40},{40,32},{48,56},{56,48},{64,72... | collective-permute-start | bytes 393224 | tf_op jit(solution)/shard_map/ppermute | solution.py:298

commit v4 on v3

--- a/solution.py
+++ b/solution.py
@@ -114,18 +114,21 @@
     )(in_hbm(grads), in_hbm(errors), in_hbm(q_t))
 
 
-def add(x, y, scale=1.0):
-    def kernel(x, y, out):
-        out[...] = (x[...] + y[...]) * scale
+def add(terms, scale=1.0):
+    def kernel(*refs):
+        values = [ref[...] for ref in refs[:-1]]
+        while len(values) > 1:
+            values = [x + y for x, y in zip(values[::2], values[1::2])]
+        refs[-1][...] = values[0] * scale
 
     return pl.pallas_call(
         kernel,
-        in_specs=[whole] * 2,
+        in_specs=[whole] * len(terms),
         out_specs=whole,
-        out_shape=pltpu.VMEM(x.shape, f32),
+        out_shape=pltpu.VMEM(terms[0].shape, f32),
         compiler_params=params,
         name="add",
-    )(in_vmem(x), in_vmem(y))
+    )(*[in_vmem(term) for term in terms])
 
 
 def right_kernel(terms, p_own, p_other, raw, gram, p_terms):
@@ -299,14 +302,13 @@
 
 
 def sum_left(other, own, scale):
-    total = add(own, swap(other, lambda x, y, core: (x, y, 1 - core)))
-    for at, (first, second) in enumerate([((1, 0), (0, 1)), ((3, 0), (0, 3)), ((0, 1), (1, 0)), ((0, 3), (3, 0))]):
-
-        def partner(x, y, core):
-            dx, dy = (first, second)[core]
-            return x ^ dx, y ^ dy, core
-
-        total = add(total, swap(total, partner), scale if at == 3 else 1.0)
+    total = add([own, swap(other, lambda x, y, core: (x, y, 1 - core))])
+    for axis, factor in (0, 1.0), (1, scale):
+        near, wrap, far = (
+            swap(total, lambda x, y, core, to=to: (x ^ to, y, core) if axis == 0 else (x, y ^ to, core))
+            for to in (1, 3, 2)
+        )
+        total = add([total, near, wrap, far], factor)
     return total, swap(total, lambda x, y, core: (x, y, 1 - core))
 
 

time: 79.4 us -> 76.5 us (0.963)
  waiting for transfers between devices: 18.1 us -> 16.1 us
    ppermute x6 -> x8, waiting for transfers between devices: 18.1 us -> 16.1 us  [swap(): return lax.ppermute(x, 'dp', pairs)]
    ppermute x6 -> x8, starting transfers between devices: 10.2 us -> 9.45 us  [swap(): return lax.ppermute(x, 'dp', pairs)]
  transfers between devices with their start and end apart: 6 -> 8, of which waited for: 6 -> 6; matrix products, arithmetic and copies ran while one was open for 0% -> 0% of each run, Pallas kernels for 0% -> 0%
where the time goes in v4:
time: 76.5 us; the launch traced here: 76.3 us
  blocking collectives  41 us (54%)
  waiting for transfers between devices  16.1 us (21%)
  starting transfers between devices  9.45 us (12%)
  Pallas kernels  9.06 us (12%)
    all_to_all x3, blocking collectives, exchange(): return lax.all_to_all(x, axis, 0, 0, tiled=True)  41 us
    ppermute x8, waiting for transfers between devices, swap(): return lax.ppermute(x, 'dp', pairs)  16.1 us
    ppermute x8, starting transfers between devices, swap(): return lax.ppermute(x, 'dp', pairs)  9.45 us
    pallas_call x1, Pallas kernels, left(): pl.pallas_call(left_kernel, in_specs=[pl.BlockSpec(memory_space=pltpu.HBM...  3.65 us
    pallas_call x1, Pallas kernels, last(): pl.pallas_call(last_kernel, in_specs=[whole] * 4, out_specs=[pl.BlockSpec...  3.5 us
  transfers between devices with their start and end apart: 8, of which 6 were waited for; matrix products, arithmetic and copies ran while one was open for 0% of the time, Pallas kernels for 0%

profile of v4, /device:TPU:1, one launch (start us, length us, event | category | flops | bytes accessed | tf_op | source)
XLA Modules:
  0.0 76.3 jit_solution(4832867291362928785)
XLA Ops:
  0.6 3.6 %left.1 = (bf16[2,2,1024,512]{3,2,1,0:T(8,128)(2,1)S(1)}, f32[8,32,128]{2,1,0:T(8,128)S(1)}, f32[8,32,128]{2,1,0:T(8,128)S(1)}) custom-call(bf16[2,1024,512]{2,1,0:T(8,128)(2,1)} %bitcast.12, f32[2,1024,512]{2,1,0:T(8,128)} %bitcast.11, f32[2,32,512]{2,1,0:T(8,128)} %bitcast.13), custom_call_target="tpu_custom_call" | custom-call | tf_op jit(solution)/shard_map/left/pallas_call | solution.py:95
  4.3 3.3 %collective-permute-start = (f32[8,32,128]{2,1,0:T(8,128)S(1)}, f32[8,32,128]{2,1,0:T(8,128)S(1)}, u32[]{:S(2)}, u32[]{:S(2)}) collective-permute-start(f32[8,32,128]{2,1,0:T(8,128)S(1)} %get-tuple-element.16), channel_id=1, source_target_pairs={{0,8},{8,0},{16,24},{24,16},{32,40},{40,32},{48,56},{56,48},{64,72... | collective-permute-start | bytes 393224 | tf_op jit(solution)/shard_map/ppermute | solution.py:301
  7.6 1.0 %collective-permute-done.refs_1_ = f32[8,32,128]{2,1,0:T(8,128)S(1)} collective-permute-done((f32[8,32,128]{2,1,0:T(8,128)S(1)}, f32[8,32,128]{2,1,0:T(8,128)S(1)}, u32[]{:S(2)}, u32[]{:S(2)}) %collective-permute-start) | collective-permute-done | bytes 131104 | tf_op jit(solution)/shard_map/ppermute | solution.py:301
  8.6 1.1 %collective-permute-start.3 = (f32[8,32,128]{2,1,0:T(8,128)S(1)}, f32[8,32,128]{2,1,0:T(8,128)S(1)}, u32[]{:S(2)}, u32[]{:S(2)}) collective-permute-start(f32[8,32,128]{2,1,0:T(8,128)S(1)} %add.3.refs_0_), channel_id=1, source_target_pairs={{0,128},{8,136},{16,144},{24,152},{32,160},{40,168},{48,176},{56,1... | collective-permute-start | bytes 393224 | tf_op jit(solution)/shard_map/ppermute | solution.py:301
  9.7 0.9 %collective-permute-start.2 = (f32[8,32,128]{2,1,0:T(8,128)S(1)}, f32[8,32,128]{2,1,0:T(8,128)S(1)}, u32[]{:S(2)}, u32[]{:S(2)}) collective-permute-start(f32[8,32,128]{2,1,0:T(8,128)S(1)} %add.3.refs_0_), channel_id=1, source_target_pairs={{0,192},{8,200},{16,208},{24,216},{32,224},{40,232},{48,240},{56,2... | collective-permute-start | bytes 393224 | tf_op jit(solution)/shard_map/ppermute | solution.py:301
  10.6 0.8 %collective-permute-start.1 = (f32[8,32,128]{2,1,0:T(8,128)S(1)}, f32[8,32,128]{2,1,0:T(8,128)S(1)}, u32[]{:S(2)}, u32[]{:S(2)}) collective-permute-start(f32[8,32,128]{2,1,0:T(8,128)S(1)} %add.3.refs_0_), channel_id=1, source_target_pairs={{0,64},{8,72},{16,80},{24,88},{32,96},{40,104},{48,112},{56,120},{... | collective-permute-start | bytes 393224 | tf_op jit(solution)/shard_map/ppermute | solution.py:301
  11.4 3.6 %collective-permute-done.3.refs_3_ = f32[8,32,128]{2,1,0:T(8,128)S(1)} collective-permute-done((f32[8,32,128]{2,1,0:T(8,128)S(1)}, f32[8,32,128]{2,1,0:T(8,128)S(1)}, u32[]{:S(2)}, u32[]{:S(2)}) %collective-permute-start.3) | collective-permute-done | bytes 131104 | tf_op jit(solution)/shard_map/ppermute | solution.py:301
  14.9 3.5 %collective-permute-done.2.refs_2_ = f32[8,32,128]{2,1,0:T(8,128)S(1)} collective-permute-done((f32[8,32,128]{2,1,0:T(8,128)S(1)}, f32[8,32,128]{2,1,0:T(8,128)S(1)}, u32[]{:S(2)}, u32[]{:S(2)}) %collective-permute-start.2) | collective-permute-done | bytes 131104 | tf_op jit(solution)/shard_map/ppermute | solution.py:301
  18.4 0.0 collective-permute-done.1.refs_1_
  18.5 0.7 collective-permute-start.6
  19.1 0.8 %collective-permute-start.5 = (f32[8,32,128]{2,1,0:T(8,128)S(1)}, f32[8,32,128]{2,1,0:T(8,128)S(1)}, u32[]{:S(2)}, u32[]{:S(2)}) collective-permute-start(f32[8,32,128]{2,1,0:T(8,128)S(1)} %add.4.refs_0_), channel_id=1, source_target_pairs={{0,48},{8,56},{16,32},{24,40},{32,16},{40,24},{48,0},{56,8},{64,11... | collective-permute-start | bytes 393224 | tf_op jit(solution)/shard_map/ppermute | solution.py:301
  19.9 1.3 %collective-permute-start.4 = (f32[8,32,128]{2,1,0:T(8,128)S(1)}, f32[8,32,128]{2,1,0:T(8,128)S(1)}, u32[]{:S(2)}, u32[]{:S(2)}) collective-permute-start(f32[8,32,128]{2,1,0:T(8,128)S(1)} %add.4.refs_0_), channel_id=1, source_target_pairs={{0,16},{8,24},{16,0},{24,8},{32,48},{40,56},{48,32},{56,40},{64,80... | collective-permute-start | bytes 393224 | tf_op jit(solution)/shard_map/ppermute | solution.py:301
  21.2 3.4 %collective-permute-done.6.refs_3_ = f32[8,32,128]{2,1,0:T(8,128)S(1)} collective-permute-done((f32[8,32,128]{2,1,0:T(8,128)S(1)}, f32[8,32,128]{2,1,0:T(8,128)S(1)}, u32[]{:S(2)}, u32[]{:S(2)}) %collective-permute-start.6) | collective-permute-done | bytes 131104 | tf_op jit(solution)/shard_map/ppermute | solution.py:301
  24.6 3.6 %collective-permute-done.5.refs_2_ = f32[8,32,128]{2,1,0:T(8,128)S(1)} collective-permute-done((f32[8,32,128]{2,1,0:T(8,128)S(1)}, f32[8,32,128]{2,1,0:T(8,128)S(1)}, u32[]{:S(2)}, u32[]{:S(2)}) %collective-permute-start.5) | collective-permute-done | bytes 131104 | tf_op jit(solution)/shard_map/ppermute | solution.py:301
  28.2 0.0 collective-permute-done.4.refs_1_
  28.3 0.7 collective-permute-start.7
  28.9 1.0 %collective-permute-done.7.p_other = f32[8,32,128]{2,1,0:T(8,128)S(1)} collective-permute-done((f32[8,32,128]{2,1,0:T(8,128)S(1)}, f32[8,32,128]{2,1,0:T(8,128)S(1)}, u32[]{:S(2)}, u32[]{:S(2)}) %collective-permute-start.7) | collective-permute-done | bytes 131104 | tf_op jit(solution)/shard_map/ppermute | solution.py:301
  29.9 1.1 %right.1 = (f32[2,4,32,128]{3,2,1,0:T(8,128)S(1)}, f32[2,8,128]{2,1,0:T(8,128)S(1)}, bf16[2,1024,128]{2,1,0:T(8,128)(2,1)S(1)}) custom-call(bf16[2,2,1024,512]{3,2,1,0:T(8,128)(2,1)S(1)} %get-tuple-element.14.terms, f32[8,32,128]{2,1,0:T(8,128)S(1)} %add.5.p_own, f32[8,32,128]{2,1,0:T(8,128)S(1)} %collective-permute-done.7.p_other), custom_call_target="tpu_custom_call" | custom-call | tf_op jit(solution)/shard_map/right/pallas_call | solution.py:153
  31.0 12.8 %all_to_all.15.raw = f32[32,8,128]{2,1,0:T(8,128)S(1)} all-to-all(f32[32,8,128]{2,1,0:T(8,128)S(1)} %bitcast.10), channel_id=1, replica_groups=mesh['dp'=32,'tensor'=8] {'dp'}, dimensions={0} | all-to-all | bytes 262144 | tf_op jit(solution)/shard_map/all_to_all | solution.py:292
  43.8 15.4 %all_to_all.16.x = f32[8,24,128]{2,1,0:T(8,128)S(1)} all-to-all(f32[8,24,128]{2,1,0:T(8,128)S(1)} %mix.1), channel_id=1, replica_groups=mesh['dp'=32,'tensor'=8] {'tensor'}, dimensions={0} | all-to-all | bytes 196608 | tf_op jit(solution)/shard_map/all_to_all | solution.py:292
  59.2 0.7 unmix.1
  60.0 12.8 %all_to_all.17 = f32[32,8,128]{2,1,0:T(8,128)S(1)} all-to-all(f32[32,8,128]{2,1,0:T(8,128)S(1)} %get-tuple-element.21), channel_id=1, replica_groups=mesh['dp'=32,'tensor'=8] {'dp'}, dimensions={0} | all-to-all | bytes 262144 | tf_op jit(solution)/shard_map/all_to_all | solution.py:292
  72.8 3.5 %last.1 = (bf16[2,1024,512]{2,1,0:T(8,128)(2,1)}, f32[2,1024,512]{2,1,0:T(8,128)}, f32[2,32,512]{2,1,0:T(8,128)}) custom-call(bf16[2,2,1024,512]{3,2,1,0:T(8,128)(2,1)S(1)} %get-tuple-element.14.terms, bf16[2,1024,128]{2,1,0:T(8,128)(2,1)S(1)} %get-tuple-element.17.p_terms, f32[2,32,32]{2,1,0:T(8,128)S(1)} %get-tuple-element.20.inverse, ...), custom_call_target="tpu_custom_call" | custom-call | tf_op jit(solution)/shard_map/last/pallas_call | solution.py:269
  (4 shorter events, 0.1 us)
Async XLA Ops:
  4.3 4.3 %collective-permute-start = (f32[8,32,128]{2,1,0:T(8,128)S(1)}, f32[8,32,128]{2,1,0:T(8,128)S(1)}, u32[]{:S(2)}, u32[]{:S(2)}) collective-permute-start(f32[8,32,128]{2,1,0:T(8,128)S(1)} %get-tuple-element.16), channel_id=1, source_target_pairs={{0,8},{8,0},{16,24},{24,16},{32,40},{40,32},{48,56},{56,48},{64,72... | collective-permute-start | bytes 393224 | tf_op jit(solution)/shard_map/ppermute | solution.py:301
  8.6 6.3 %collective-permute-start.3 = (f32[8,32,128]{2,1,0:T(8,128)S(1)}, f32[8,32,128]{2,1,0:T(8,128)S(1)}, u32[]{:S(2)}, u32[]{:S(2)}) collective-permute-start(f32[8,32,128]{2,1,0:T(8,128)S(1)} %add.3.refs_0_), channel_id=1, source_target_pairs={{0,128},{8,136},{16,144},{24,152},{32,160},{40,168},{48,176},{56,1... | collective-permute-start | bytes 393224 | tf_op jit(solution)/shard_map/ppermute | solution.py:301
  9.7 8.7 %collective-permute-start.2 = (f32[8,32,128]{2,1,0:T(8,128)S(1)}, f32[8,32,128]{2,1,0:T(8,128)S(1)}, u32[]{:S(2)}, u32[]{:S(2)}) collective-permute-start(f32[8,32,128]{2,1,0:T(8,128)S(1)} %add.3.refs_0_), channel_id=1, source_target_pairs={{0,192},{8,200},{16,208},{24,216},{32,224},{40,232},{48,240},{56,2... | collective-permute-start | bytes 393224 | tf_op jit(solution)/shard_map/ppermute | solution.py:301
  10.6 7.9 %collective-permute-start.1 = (f32[8,32,128]{2,1,0:T(8,128)S(1)}, f32[8,32,128]{2,1,0:T(8,128)S(1)}, u32[]{:S(2)}, u32[]{:S(2)}) collective-permute-start(f32[8,32,128]{2,1,0:T(8,128)S(1)} %add.3.refs_0_), channel_id=1, source_target_pairs={{0,64},{8,72},{16,80},{24,88},{32,96},{40,104},{48,112},{56,120},{... | collective-permute-start | bytes 393224 | tf_op jit(solution)/shard_map/ppermute | solution.py:301
  18.5 6.2 %collective-permute-start.6 = (f32[8,32,128]{2,1,0:T(8,128)S(1)}, f32[8,32,128]{2,1,0:T(8,128)S(1)}, u32[]{:S(2)}, u32[]{:S(2)}) collective-permute-start(f32[8,32,128]{2,1,0:T(8,128)S(1)} %add.4.refs_0_), channel_id=1, source_target_pairs={{0,32},{8,40},{16,48},{24,56},{32,0},{40,8},{48,16},{56,24},{64,96... | collective-permute-start | bytes 393224 | tf_op jit(solution)/shard_map/ppermute | solution.py:301
  19.1 9.1 %collective-permute-start.5 = (f32[8,32,128]{2,1,0:T(8,128)S(1)}, f32[8,32,128]{2,1,0:T(8,128)S(1)}, u32[]{:S(2)}, u32[]{:S(2)}) collective-permute-start(f32[8,32,128]{2,1,0:T(8,128)S(1)} %add.4.refs_0_), channel_id=1, source_target_pairs={{0,48},{8,56},{16,32},{24,40},{32,16},{40,24},{48,0},{56,8},{64,11... | collective-permute-start | bytes 393224 | tf_op jit(solution)/shard_map/ppermute | solution.py:301
  19.9 8.3 %collective-permute-start.4 = (f32[8,32,128]{2,1,0:T(8,128)S(1)}, f32[8,32,128]{2,1,0:T(8,128)S(1)}, u32[]{:S(2)}, u32[]{:S(2)}) collective-permute-start(f32[8,32,128]{2,1,0:T(8,128)S(1)} %add.4.refs_0_), channel_id=1, source_target_pairs={{0,16},{8,24},{16,0},{24,8},{32,48},{40,56},{48,32},{56,40},{64,80... | collective-permute-start | bytes 393224 | tf_op jit(solution)/shard_map/ppermute | solution.py:301
  28.3 1.6 %collective-permute-start.7 = (f32[8,32,128]{2,1,0:T(8,128)S(1)}, f32[8,32,128]{2,1,0:T(8,128)S(1)}, u32[]{:S(2)}, u32[]{:S(2)}) collective-permute-start(f32[8,32,128]{2,1,0:T(8,128)S(1)} %add.5.p_own), channel_id=1, source_target_pairs={{0,8},{8,0},{16,24},{24,16},{32,40},{40,32},{48,56},{56,48},{64,72... | collective-permute-start | bytes 393224 | tf_op jit(solution)/shard_map/ppermute | solution.py:301

commit v5 on v4

--- a/solution.py
+++ b/solution.py
@@ -9,6 +9,7 @@
 f32, bf16 = jnp.float32, jnp.bfloat16
 block_rows = 512
 ahead = 3
+last_pieces = {True: [(0, 256), (256, 512), (512, 1024)], False: [(0, 512), (512, 1024)]}
 
 
 def halves(x):
@@ -52,7 +53,7 @@
     return pltpu.with_memory_space_constraint(x, pltpu.HBM)
 
 
-def left_kernel(grads, errors, q_t, terms, other, own, grads_here, errors_here, q_here, q_sem, grads_sem, errors_sem):
+def left_kernel(grads, errors, q_t, terms, merged_other, other, own, grads_here, errors_here, q_here, q_sem, grads_sem, errors_sem):
     layers, _, rows, _ = terms.shape
     core = this_core()
     pieces = [(l, b) for l in (1 - core, core) for b in range(rows // block_rows)]
@@ -79,6 +80,8 @@
                 copy.start()
         at = pl.ds(b * block_rows, block_rows)
         merged = grads_here[l, at].astype(f32) + errors_here[l, at]
+        if n < len(pieces) // 2:
+            merged_other[at] = merged
         merged_high, merged_low = halves(merged)
         terms[l, 0, at] = merged_high
         terms[l, 1, at] = merged_low
@@ -95,9 +98,10 @@
     return pl.pallas_call(
         left_kernel,
         in_specs=[pl.BlockSpec(memory_space=pltpu.HBM)] * 3,
-        out_specs=[whole] * 3,
+        out_specs=[whole] * 4,
         out_shape=[
             pltpu.VMEM((layers, 2, rows, cols), bf16),
+            pltpu.VMEM((rows, cols), f32),
             pltpu.VMEM((rows // 128, rank, 128), f32),
             pltpu.VMEM((rows // 128, rank, 128), f32),
         ],
@@ -131,53 +135,77 @@
     )(*[in_vmem(term) for term in terms])
 
 
-def right_kernel(terms, p_own, p_other, raw, gram, p_terms):
-    layers = terms.shape[0]
-    tiles, rank, _ = p_own.shape
-    core = this_core()
-    for l in range(layers):
-        factor = jnp.concatenate([jnp.where(core == l, p_own[at], p_other[at]) for at in range(tiles)], 1)
-        small = thirds(factor)
-        term = split_dot(small, terms[l, 0], terms[l, 1], ((1,), (0,)))
-        for at in range(raw.shape[1]):
-            raw[l, at] = term[:, at * 128 : (at + 1) * 128]
-        square = dot(factor, factor, ((1,), (1,)), highest)
-        gram[l] = jnp.concatenate([square[at : at + 8] for at in range(0, rank, 8)], 1)
-        stack = jnp.concatenate([small[0], small[1], small[0], jnp.zeros_like(small[0])], 0)
-        p_terms[l] = stack.T
-
-
-def right(terms, p_own, p_other):
-    layers, _, rows, cols = terms.shape
-    rank = p_own.shape[1]
-    return pl.pallas_call(
-        right_kernel,
-        in_specs=[whole] * 3,
-        out_specs=[whole] * 3,
-        out_shape=[
-            pltpu.VMEM((layers, cols // 128, rank, 128), f32),
-            pltpu.VMEM((layers, 8, 128), f32),
-            pltpu.VMEM((layers, rows, 4 * rank), bf16),
-        ],
-        compiler_params=params,
-        name="right",
-    )(in_vmem(terms), in_vmem(p_own), in_vmem(p_other))
-
-
-def mix(raw, gram, copies):
-    def kernel(raw, gram, out):
-        total = jnp.sum(raw[...], axis=0)
-        both = jnp.concatenate([total, gram[0], gram[1]], 0)
-        out[...] = jnp.broadcast_to(both[None], out.shape)
+def pair(terms, merged):
+    _, _, rows, cols = terms.shape
+
+    def kernel(terms, merged, out):
+        core = this_core()
+        both = (terms[core, 0].astype(f32) + terms[core, 1].astype(f32)) + merged[...]
+        out[0], out[1] = halves(both)
 
     return pl.pallas_call(
         kernel,
         in_specs=[whole] * 2,
         out_specs=whole,
-        out_shape=pltpu.VMEM((copies, raw.shape[1] + 16, 128), f32),
+        out_shape=pltpu.VMEM((2, rows, cols), bf16),
+        compiler_params=params,
+        cost_estimate=pl.CostEstimate(flops=4_000_000, bytes_accessed=6 * 1024 * 1024, transcendentals=0),
+        name="pair",
+    )(in_vmem(terms), in_vmem(merged))
+
+
+def stack_terms(one, two):
+    return jnp.concatenate([one, two, one, jnp.zeros_like(one)], 0).T
+
+
+def packed_gram(factor):
+    rank = factor.shape[0]
+    square = dot(factor, factor, ((1,), (1,)), highest)
+    return jnp.concatenate([square[at : at + 8] for at in range(0, rank, 8)], 1)
+
+
+def right_kernel(pair_terms, p_t, raw, gram, p_terms):
+    tiles, rank, _ = p_t.shape
+    factor = jnp.concatenate([p_t[at] for at in range(tiles)], 1)
+    small = thirds(factor)
+    term = split_dot(small, pair_terms[0], pair_terms[1], ((1,), (0,)))
+    for at in range(raw.shape[0]):
+        raw[at] = term[:, at * 128 : (at + 1) * 128]
+    gram[...] = packed_gram(factor)
+    p_terms[...] = stack_terms(*small[:2])
+
+
+def right(pair_terms, p_t):
+    _, rows, cols = pair_terms.shape
+    rank = p_t.shape[1]
+    return pl.pallas_call(
+        right_kernel,
+        in_specs=[whole] * 2,
+        out_specs=[whole] * 3,
+        out_shape=[
+            pltpu.VMEM((cols // 128, rank, 128), f32),
+            pltpu.VMEM((8, 128), f32),
+            pltpu.VMEM((rows, 4 * rank), bf16),
+        ],
+        compiler_params=params,
+        name="right",
+    )(in_vmem(pair_terms), in_vmem(p_t))
+
+
+def mix(raw, gram, p_other, copies):
+    def kernel(raw, gram, p_other, out):
+        factor = jnp.concatenate([p_other[at] for at in range(p_other.shape[0])], 1)
+        both = jnp.concatenate([jnp.sum(raw[...], axis=0), gram[...], packed_gram(factor)], 0)
+        out[...] = jnp.broadcast_to(both[None], out.shape)
+
+    return pl.pallas_call(
+        kernel,
+        in_specs=[whole] * 3,
+        out_specs=whole,
+        out_shape=pltpu.VMEM((copies, 24, 128), f32),
         compiler_params=params,
         name="mix",
-    )(in_vmem(raw), in_vmem(gram))
+    )(in_vmem(raw), in_vmem(gram), in_vmem(p_other))
 
 
 def lower_inverses(packed, rank):
@@ -231,10 +259,12 @@
 
 
 def last_kernel(
-    terms, p_terms, inverse, raw, decompressed, new_errors, q_new,
+    terms, p_terms, p_other, inverse, raw, decompressed, new_errors, q_new,
     decompressed_here, errors_here, q_here, decompressed_sem, errors_sem, q_sem,
 ):
-    layers, _, rows, _ = terms.shape
+    _, _, rows, cols = terms.shape
+    rank = inverse.shape[1]
+    core = this_core()
     copies = []
 
     def send(source, target, sem):
@@ -242,33 +272,41 @@
         copy.start()
         copies.append(copy)
 
-    for l in range(layers):
-        sums = jnp.concatenate([raw[l, at] for at in range(raw.shape[1])], 1)
-        q = dot(inverse[l], sums, ((1,), (0,)), highest)
+    for own in (True, False):
+        l = core if own else 1 - core
+        lower = inverse[0 if own else 1]
+        lanes = [[raw[2 * (j * rank // 8 + i) + l] for i in range(rank // 8)] for j in range(cols // 128)]
+        sums = jnp.concatenate([jnp.concatenate(tiles, 0) for tiles in lanes], 1)
+        q = dot(lower, sums, ((1,), (0,)), highest)
         q_here[l] = q
-        send(q_here.at[l], q_new.at[l], q_sem.at[l])
-        right_high, right_low = halves(dot(inverse[l], q, ((0,), (0,)), highest))
+        send(q_here.at[l], q_new.at[l], q_sem.at[0 if own else 1])
+        right_high, right_low = halves(dot(lower, q, ((0,), (0,)), highest))
         stack = jnp.concatenate([right_high, right_high, right_low, jnp.zeros_like(right_high)], 0)
-        for b in range(rows // block_rows):
-            at = pl.ds(b * block_rows, block_rows)
-            n = l * (rows // block_rows) + b
-            approx = dot(p_terms[l, at], stack, ((1,), (0,)))
+        for n, (start, end) in enumerate(last_pieces[own]):
+            at = pl.ds(start, end - start)
+            if own:
+                left_rows = p_terms[at]
+            else:
+                tiles = [p_other[tile] for tile in range(start // 128, end // 128)]
+                left_rows = stack_terms(*halves(jnp.concatenate(tiles, 1)))
+            approx = dot(left_rows, stack, ((1,), (0,)))
             decompressed_here[l, at] = approx.astype(bf16)
             errors_here[l, at] = (terms[l, 0, at].astype(f32) + terms[l, 1, at].astype(f32)) - approx
-            send(decompressed_here.at[l, at], decompressed.at[l, at], decompressed_sem.at[n])
-            send(errors_here.at[l, at], new_errors.at[l, at], errors_sem.at[n])
+            sem = n if own else len(last_pieces[True]) + n
+            send(decompressed_here.at[l, at], decompressed.at[l, at], decompressed_sem.at[sem])
+            send(errors_here.at[l, at], new_errors.at[l, at], errors_sem.at[sem])
     for copy in copies:
         copy.wait()
 
 
-def last(terms, p_terms, inverse, raw):
+def last(terms, p_terms, p_other, inverse, raw):
     layers, _, rows, cols = terms.shape
     shape = (layers, rows, cols)
     rank = inverse.shape[1]
-    pieces = layers * rows // block_rows
+    pieces = len(last_pieces[True]) + len(last_pieces[False])
     return pl.pallas_call(
         last_kernel,
-        in_specs=[whole] * 4,
+        in_specs=[whole] * 5,
         out_specs=[pl.BlockSpec(memory_space=pltpu.HBM)] * 3,
         out_shape=[
             pltpu.HBM(shape, bf16),
@@ -285,11 +323,11 @@
         ],
         compiler_params=params,
         name="last",
-    )(in_vmem(terms), in_vmem(p_terms), in_vmem(inverse), in_vmem(raw))
-
-
-def exchange(x, axis):
-    return lax.all_to_all(x, axis, 0, 0, tiled=True)
+    )(*[in_vmem(x) for x in (terms, p_terms, p_other, inverse, raw)])
+
+
+def exchange(x, axis, groups=None):
+    return lax.all_to_all(x, axis, 0, 0, axis_index_groups=groups, tiled=True)
 
 
 def swap(x, partner):
@@ -301,27 +339,31 @@
     return lax.ppermute(x, "dp", pairs)
 
 
-def sum_left(other, own, scale):
-    total = add([own, swap(other, lambda x, y, core: (x, y, 1 - core))])
-    for axis, factor in (0, 1.0), (1, scale):
-        near, wrap, far = (
-            swap(total, lambda x, y, core, to=to: (x ^ to, y, core) if axis == 0 else (x, y ^ to, core))
-            for to in (1, 3, 2)
-        )
-        total = add([total, near, wrap, far], factor)
-    return total, swap(total, lambda x, y, core: (x, y, 1 - core))
+def swap_cores(x):
+    return swap(x, lambda x, y, core: (x, y, 1 - core))
+
+
+def sum_axis(total, axis, scale):
+    near, wrap, far = (
+        swap(total, lambda x, y, core, to=to: (x ^ to, y, core) if axis == 0 else (x, y ^ to, core))
+        for to in (1, 3, 2)
+    )
+    return add([total, near, wrap, far], scale)
 
 
 def on_device(grads, errors, q_prev):
     replicas, slabs, rank = lax.axis_size("dp"), lax.axis_size("tensor"), q_prev.shape[2]
-    terms, other, own = left(grads[:, 0], errors[:, 0], jnp.swapaxes(q_prev, 1, 2))
-    raw, gram, p_terms = right(terms, *sum_left(other, own, 1.0 / replicas))
-    raw_shape = raw.shape
-    raw = exchange(raw.reshape(replicas, -1, 128), "dp")
-    both = exchange(mix(raw, gram, slabs), "tensor")
+    terms, merged, other, own = left(grads[:, 0], errors[:, 0], jnp.swapaxes(q_prev, 1, 2))
+    total, merged = lax.optimization_barrier((add([own, swap_cores(other)]), merged))
+    pair_terms = pair(terms, swap_cores(merged))
+    p_t = sum_axis(sum_axis(total, 0, 1.0), 1, 1.0 / replicas)
+    raw, gram, p_terms = right(pair_terms, p_t)
+    raw, p_other = lax.optimization_barrier((raw, swap_cores(p_t)))
+    chips = [[2 * chip + core for chip in range(replicas // 2)] for core in range(2)]
+    raw = exchange(raw.reshape(replicas // 2, 8, 128), "dp", chips)
+    both = exchange(mix(raw, gram, p_other, slabs), "tensor")
     raw, inverse = unmix(both, replicas, rank, 1.0 / replicas)
-    raw = exchange(raw, "dp").reshape(raw_shape)
-    decompressed, new_errors, q_new = last(terms, p_terms, inverse, raw)
+    decompressed, new_errors, q_new = last(terms, p_terms, p_other, inverse, exchange(raw, "dp"))
     return decompressed, new_errors[:, None], jnp.swapaxes(q_new, 1, 2)
 
 

time: 76.5 us -> 75.6 us (0.988)
  waiting for transfers between devices: 16.1 us -> 15.1 us
    ppermute x8 -> x9, waiting for transfers between devices: 16.1 us -> 15.1 us  [swap(): return lax.ppermute(x, 'dp', pairs)]
    ppermute x8 -> x9, starting transfers between devices: 9.45 us -> 9.8 us  [swap(): return lax.ppermute(x, 'dp', pairs)]
    pallas_call x3 -> x4, Pallas kernels: 4.61 us -> 4.89 us  [the longest x1 3.42 us: last(): pl.pallas_call(last_kernel, in_specs=[whole] * 5, out_specs=[pl.BlockSpec...]
  transfers between devices with their start and end apart: 8 -> 9, of which waited for: 6 -> 5; matrix products, arithmetic and copies ran while one was open for 0% -> 0% of each run, Pallas kernels for 0% -> 2%
where the time goes in v5:
time: 75.6 us; the launch traced here: 75.4 us
  blocking collectives  40.4 us (53%)
  waiting for transfers between devices  15.1 us (20%)
  starting transfers between devices  9.8 us (13%)
  Pallas kernels  9.33 us (12%)
    all_to_all x3, blocking collectives, exchange(): return lax.all_to_all(x, axis, 0, 0, axis_index_groups=groups, tiled=True)  40.4 us
    ppermute x9, waiting for transfers between devices, swap(): return lax.ppermute(x, 'dp', pairs)  15.1 us
    ppermute x9, starting transfers between devices, swap(): return lax.ppermute(x, 'dp', pairs)  9.8 us
    pallas_call x1, Pallas kernels, left(): pl.pallas_call(left_kernel, in_specs=[pl.BlockSpec(memory_space=pltpu.HBM...  3.64 us
    pallas_call x1, Pallas kernels, last(): pl.pallas_call(last_kernel, in_specs=[whole] * 5, out_specs=[pl.BlockSpec...  3.42 us
  transfers between devices with their start and end apart: 9, of which 5 were waited for; matrix products, arithmetic and copies ran while one was open for 0% of the time, Pallas kernels for 2%

profile of v5, /device:TPU:1, one launch (start us, length us, event | category | flops | bytes accessed | tf_op | source)
XLA Modules:
  0.0 75.4 jit_solution(11841144594300225267)
XLA Ops:
  0.6 3.6 %left.1 = (bf16[2,2,1024,512]{3,2,1,0:T(8,128)(2,1)S(1)}, f32[1024,512]{1,0:T(8,128)S(1)}, f32[8,32,128]{2,1,0:T(8,128)S(1)}, f32[8,32,128]{2,1,0:T(8,128)S(1)}) custom-call(bf16[2,1024,512]{2,1,0:T(8,128)(2,1)} %bitcast.10, f32[2,1024,512]{2,1,0:T(8,128)} %bitcast.9, f32[2,32,512]{2,1,0:T(8,128)} %bitcast.11), custom_call_target="tpu_custom_call" | custom-call | tf_op jit(solution)/shard_map/left/pallas_call | solution.py:98
  4.3 3.3 %collective-permute-start = (f32[8,32,128]{2,1,0:T(8,128)S(1)}, f32[8,32,128]{2,1,0:T(8,128)S(1)}, u32[]{:S(2)}, u32[]{:S(2)}) collective-permute-start(f32[8,32,128]{2,1,0:T(8,128)S(1)} %get-tuple-element.21), channel_id=1, source_target_pairs={{0,8},{8,0},{16,24},{24,16},{32,40},{40,32},{48,56},{56,48},{64,72... | collective-permute-start | bytes 393224 | tf_op jit(solution)/shard_map/ppermute | solution.py:339
  7.6 1.0 %collective-permute-done.refs_1_ = f32[8,32,128]{2,1,0:T(8,128)S(1)} collective-permute-done((f32[8,32,128]{2,1,0:T(8,128)S(1)}, f32[8,32,128]{2,1,0:T(8,128)S(1)}, u32[]{:S(2)}, u32[]{:S(2)}) %collective-permute-start) | collective-permute-done | bytes 131104 | tf_op jit(solution)/shard_map/ppermute | solution.py:339
  8.6 0.4 collective-permute-start.1
  9.1 1.0 %collective-permute-start.4 = (f32[8,32,128]{2,1,0:T(8,128)S(1)}, f32[8,32,128]{2,1,0:T(8,128)S(1)}, u32[]{:S(2)}, u32[]{:S(2)}) collective-permute-start(f32[8,32,128]{2,1,0:T(8,128)S(1)} %add.3.refs_0_), channel_id=1, source_target_pairs={{0,128},{8,136},{16,144},{24,152},{32,160},{40,168},{48,176},{56,1... | collective-permute-start | bytes 393224 | tf_op jit(solution)/shard_map/ppermute | solution.py:339
  10.1 0.9 %collective-permute-start.3 = (f32[8,32,128]{2,1,0:T(8,128)S(1)}, f32[8,32,128]{2,1,0:T(8,128)S(1)}, u32[]{:S(2)}, u32[]{:S(2)}) collective-permute-start(f32[8,32,128]{2,1,0:T(8,128)S(1)} %add.3.refs_0_), channel_id=1, source_target_pairs={{0,192},{8,200},{16,208},{24,216},{32,224},{40,232},{48,240},{56,2... | collective-permute-start | bytes 393224 | tf_op jit(solution)/shard_map/ppermute | solution.py:339
  10.9 0.8 %collective-permute-start.2 = (f32[8,32,128]{2,1,0:T(8,128)S(1)}, f32[8,32,128]{2,1,0:T(8,128)S(1)}, u32[]{:S(2)}, u32[]{:S(2)}) collective-permute-start(f32[8,32,128]{2,1,0:T(8,128)S(1)} %add.3.refs_0_), channel_id=1, source_target_pairs={{0,64},{8,72},{16,80},{24,88},{32,96},{40,104},{48,112},{56,120},{... | collective-permute-start | bytes 393224 | tf_op jit(solution)/shard_map/ppermute | solution.py:339
  11.7 3.8 %collective-permute-done.4.refs_3_ = f32[8,32,128]{2,1,0:T(8,128)S(1)} collective-permute-done((f32[8,32,128]{2,1,0:T(8,128)S(1)}, f32[8,32,128]{2,1,0:T(8,128)S(1)}, u32[]{:S(2)}, u32[]{:S(2)}) %collective-permute-start.4) | collective-permute-done | bytes 131104 | tf_op jit(solution)/shard_map/ppermute | solution.py:339
  15.5 3.3 %collective-permute-done.3.refs_2_ = f32[8,32,128]{2,1,0:T(8,128)S(1)} collective-permute-done((f32[8,32,128]{2,1,0:T(8,128)S(1)}, f32[8,32,128]{2,1,0:T(8,128)S(1)}, u32[]{:S(2)}, u32[]{:S(2)}) %collective-permute-start.3) | collective-permute-done | bytes 131104 | tf_op jit(solution)/shard_map/ppermute | solution.py:339
  18.8 0.0 collective-permute-done.2.refs_1_
  18.8 0.9 %collective-permute-start.7 = (f32[8,32,128]{2,1,0:T(8,128)S(1)}, f32[8,32,128]{2,1,0:T(8,128)S(1)}, u32[]{:S(2)}, u32[]{:S(2)}) collective-permute-start(f32[8,32,128]{2,1,0:T(8,128)S(1)} %add.4.refs_0_), channel_id=1, source_target_pairs={{0,32},{8,40},{16,48},{24,56},{32,0},{40,8},{48,16},{56,24},{64,96... | collective-permute-start | bytes 393224 | tf_op jit(solution)/shard_map/ppermute | solution.py:339
  19.7 0.8 %collective-permute-start.6 = (f32[8,32,128]{2,1,0:T(8,128)S(1)}, f32[8,32,128]{2,1,0:T(8,128)S(1)}, u32[]{:S(2)}, u32[]{:S(2)}) collective-permute-start(f32[8,32,128]{2,1,0:T(8,128)S(1)} %add.4.refs_0_), channel_id=1, source_target_pairs={{0,48},{8,56},{16,32},{24,40},{32,16},{40,24},{48,0},{56,8},{64,11... | collective-permute-start | bytes 393224 | tf_op jit(solution)/shard_map/ppermute | solution.py:339
  20.5 1.1 %collective-permute-start.5 = (f32[8,32,128]{2,1,0:T(8,128)S(1)}, f32[8,32,128]{2,1,0:T(8,128)S(1)}, u32[]{:S(2)}, u32[]{:S(2)}) collective-permute-start(f32[8,32,128]{2,1,0:T(8,128)S(1)} %add.4.refs_0_), channel_id=1, source_target_pairs={{0,16},{8,24},{16,0},{24,8},{32,48},{40,56},{48,32},{56,40},{64,80... | collective-permute-start | bytes 393224 | tf_op jit(solution)/shard_map/ppermute | solution.py:339
  21.6 3.4 %collective-permute-done.7.refs_3_ = f32[8,32,128]{2,1,0:T(8,128)S(1)} collective-permute-done((f32[8,32,128]{2,1,0:T(8,128)S(1)}, f32[8,32,128]{2,1,0:T(8,128)S(1)}, u32[]{:S(2)}, u32[]{:S(2)}) %collective-permute-start.7) | collective-permute-done | bytes 131104 | tf_op jit(solution)/shard_map/ppermute | solution.py:339
  25.0 3.6 %collective-permute-done.6.refs_2_ = f32[8,32,128]{2,1,0:T(8,128)S(1)} collective-permute-done((f32[8,32,128]{2,1,0:T(8,128)S(1)}, f32[8,32,128]{2,1,0:T(8,128)S(1)}, u32[]{:S(2)}, u32[]{:S(2)}) %collective-permute-start.6) | collective-permute-done | bytes 131104 | tf_op jit(solution)/shard_map/ppermute | solution.py:339
  28.6 0.6 collective-permute-start.8
  29.3 0.5 pair.1.pair_terms
  29.8 0.6 right.1
  30.5 10.9 %all_to_all.15.raw = f32[16,8,128]{2,1,0:T(8,128)S(1)} all-to-all(f32[16,8,128]{2,1,0:T(8,128)S(1)} %bitcast.8), channel_id=1, replica_groups={{0,16,32,48,64,80,96,112,128,144,160,176,192,208,224,240},{8,24,40,56,7..., dimensions={0} | all-to-all | bytes 131072 | tf_op jit(solution)/shard_map/all_to_all | solution.py:330
  41.3 0.3 mix.1
  41.7 15.7 %all_to_all.16.x = f32[8,24,128]{2,1,0:T(8,128)S(1)} all-to-all(f32[8,24,128]{2,1,0:T(8,128)S(1)} %mix.1), channel_id=1, replica_groups=mesh['dp'=32,'tensor'=8] {'tensor'}, dimensions={0} | all-to-all | bytes 196608 | tf_op jit(solution)/shard_map/all_to_all | solution.py:330
  57.3 0.7 unmix.1
  58.1 13.9 %all_to_all.17.raw = f32[32,8,128]{2,1,0:T(8,128)S(1)} all-to-all(f32[32,8,128]{2,1,0:T(8,128)S(1)} %get-tuple-element.31), channel_id=1, replica_groups=mesh['dp'=32,'tensor'=8] {'dp'}, dimensions={0} | all-to-all | bytes 262144 | tf_op jit(solution)/shard_map/all_to_all | solution.py:330
  71.9 3.4 %last.1 = (bf16[2,1024,512]{2,1,0:T(8,128)(2,1)}, f32[2,1024,512]{2,1,0:T(8,128)}, f32[2,32,512]{2,1,0:T(8,128)}) custom-call(bf16[2,2,1024,512]{3,2,1,0:T(8,128)(2,1)S(1)} %get-tuple-element.19.terms, bf16[1024,128]{1,0:T(8,128)(2,1)S(1)} %get-tuple-element.25.p_terms, f32[8,32,128]{2,1,0:T(8,128)S(1)} %collective-permute-done.8.p_other, ...), custom_call_target="tpu_custom_call" | custom-call | tf_op jit(solution)/shard_map/last/pallas_call | solution.py:307
  (6 shorter events, 0.1 us)
Async XLA Ops:
  4.3 4.3 %collective-permute-start = (f32[8,32,128]{2,1,0:T(8,128)S(1)}, f32[8,32,128]{2,1,0:T(8,128)S(1)}, u32[]{:S(2)}, u32[]{:S(2)}) collective-permute-start(f32[8,32,128]{2,1,0:T(8,128)S(1)} %get-tuple-element.21), channel_id=1, source_target_pairs={{0,8},{8,0},{16,24},{24,16},{32,40},{40,32},{48,56},{56,48},{64,72... | collective-permute-start | bytes 393224 | tf_op jit(solution)/shard_map/ppermute | solution.py:339
  8.6 20.7 %collective-permute-start.1 = (f32[1024,512]{1,0:T(8,128)S(1)}, f32[1024,512]{1,0:T(8,128)S(1)}, u32[]{:S(2)}, u32[]{:S(2)}) collective-permute-start(f32[1024,512]{1,0:T(8,128)S(1)} %get-tuple-element.23), channel_id=1, source_target_pairs={{0,8},{8,0},{16,24},{24,16},{32,40},{40,32},{48,56},{56,48},{64,72... | collective-permute-start | bytes 6291464 | tf_op jit(solution)/shard_map/ppermute | solution.py:339
  9.1 6.5 %collective-permute-start.4 = (f32[8,32,128]{2,1,0:T(8,128)S(1)}, f32[8,32,128]{2,1,0:T(8,128)S(1)}, u32[]{:S(2)}, u32[]{:S(2)}) collective-permute-start(f32[8,32,128]{2,1,0:T(8,128)S(1)} %add.3.refs_0_), channel_id=1, source_target_pairs={{0,128},{8,136},{16,144},{24,152},{32,160},{40,168},{48,176},{56,1... | collective-permute-start | bytes 393224 | tf_op jit(solution)/shard_map/ppermute | solution.py:339
  10.1 8.7 %collective-permute-start.3 = (f32[8,32,128]{2,1,0:T(8,128)S(1)}, f32[8,32,128]{2,1,0:T(8,128)S(1)}, u32[]{:S(2)}, u32[]{:S(2)}) collective-permute-start(f32[8,32,128]{2,1,0:T(8,128)S(1)} %add.3.refs_0_), channel_id=1, source_target_pairs={{0,192},{8,200},{16,208},{24,216},{32,224},{40,232},{48,240},{56,2... | collective-permute-start | bytes 393224 | tf_op jit(solution)/shard_map/ppermute | solution.py:339
  10.9 7.9 %collective-permute-start.2 = (f32[8,32,128]{2,1,0:T(8,128)S(1)}, f32[8,32,128]{2,1,0:T(8,128)S(1)}, u32[]{:S(2)}, u32[]{:S(2)}) collective-permute-start(f32[8,32,128]{2,1,0:T(8,128)S(1)} %add.3.refs_0_), channel_id=1, source_target_pairs={{0,64},{8,72},{16,80},{24,88},{32,96},{40,104},{48,112},{56,120},{... | collective-permute-start | bytes 393224 | tf_op jit(solution)/shard_map/ppermute | solution.py:339
  18.8 6.2 %collective-permute-start.7 = (f32[8,32,128]{2,1,0:T(8,128)S(1)}, f32[8,32,128]{2,1,0:T(8,128)S(1)}, u32[]{:S(2)}, u32[]{:S(2)}) collective-permute-start(f32[8,32,128]{2,1,0:T(8,128)S(1)} %add.4.refs_0_), channel_id=1, source_target_pairs={{0,32},{8,40},{16,48},{24,56},{32,0},{40,8},{48,16},{56,24},{64,96... | collective-permute-start | bytes 393224 | tf_op jit(solution)/shard_map/ppermute | solution.py:339
  19.7 8.9 %collective-permute-start.6 = (f32[8,32,128]{2,1,0:T(8,128)S(1)}, f32[8,32,128]{2,1,0:T(8,128)S(1)}, u32[]{:S(2)}, u32[]{:S(2)}) collective-permute-start(f32[8,32,128]{2,1,0:T(8,128)S(1)} %add.4.refs_0_), channel_id=1, source_target_pairs={{0,48},{8,56},{16,32},{24,40},{32,16},{40,24},{48,0},{56,8},{64,11... | collective-permute-start | bytes 393224 | tf_op jit(solution)/shard_map/ppermute | solution.py:339
  20.5 8.1 %collective-permute-start.5 = (f32[8,32,128]{2,1,0:T(8,128)S(1)}, f32[8,32,128]{2,1,0:T(8,128)S(1)}, u32[]{:S(2)}, u32[]{:S(2)}) collective-permute-start(f32[8,32,128]{2,1,0:T(8,128)S(1)} %add.4.refs_0_), channel_id=1, source_target_pairs={{0,16},{8,24},{16,0},{24,8},{32,48},{40,56},{48,32},{56,40},{64,80... | collective-permute-start | bytes 393224 | tf_op jit(solution)/shard_map/ppermute | solution.py:339
  28.6 1.8 %collective-permute-start.8 = (f32[8,32,128]{2,1,0:T(8,128)S(1)}, f32[8,32,128]{2,1,0:T(8,128)S(1)}, u32[]{:S(2)}, u32[]{:S(2)}) collective-permute-start(f32[8,32,128]{2,1,0:T(8,128)S(1)} %add.5.p_t), channel_id=1, source_target_pairs={{0,8},{8,0},{16,24},{24,16},{32,40},{40,32},{48,56},{56,48},{64,72... | collective-permute-start | bytes 393224 | tf_op jit(solution)/shard_map/ppermute | solution.py:339

commit v6 on v5

--- a/solution.py
+++ b/solution.py
@@ -343,9 +343,9 @@
     return swap(x, lambda x, y, core: (x, y, 1 - core))
 
 
-def sum_axis(total, axis, scale):
+def sum_axis(total, turn, scale):
     near, wrap, far = (
-        swap(total, lambda x, y, core, to=to: (x ^ to, y, core) if axis == 0 else (x, y ^ to, core))
+        swap(total, lambda x, y, core, to=to: (x ^ to, y, core) if core == turn else (x, y ^ to, core))
         for to in (1, 3, 2)
     )
     return add([total, near, wrap, far], scale)

time: 75.6 us -> 72.6 us (0.960)
  waiting for transfers between devices: 15.1 us -> 9.65 us
  starting transfers between devices: 9.8 us -> 12.3 us
    ppermute x9, waiting for transfers between devices: 15.1 us -> 9.65 us  [swap(): return lax.ppermute(x, 'dp', pairs)]
    ppermute x9, starting transfers between devices: 9.8 us -> 12.3 us  [swap(): return lax.ppermute(x, 'dp', pairs)]
where the time goes in v6:
time: 72.6 us; the launch traced here: 72.4 us
  blocking collectives  40.5 us (56%)
  starting transfers between devices  12.3 us (17%)
  waiting for transfers between devices  9.65 us (13%)
  Pallas kernels  9.33 us (13%)
    all_to_all x3, blocking collectives, exchange(): return lax.all_to_all(x, axis, 0, 0, axis_index_groups=groups, tiled=True)  40.5 us
    ppermute x9, starting transfers between devices, swap(): return lax.ppermute(x, 'dp', pairs)  12.3 us
    ppermute x9, waiting for transfers between devices, swap(): return lax.ppermute(x, 'dp', pairs)  9.65 us
    pallas_call x1, Pallas kernels, left(): pl.pallas_call(left_kernel, in_specs=[pl.BlockSpec(memory_space=pltpu.HBM...  3.64 us
    pallas_call x1, Pallas kernels, last(): pl.pallas_call(last_kernel, in_specs=[whole] * 5, out_specs=[pl.BlockSpec...  3.42 us
  transfers between devices with their start and end apart: 9, of which 5 were waited for; matrix products, arithmetic and copies ran while one was open for 0% of the time, Pallas kernels for 2%

profile of v6, /device:TPU:1, one launch (start us, length us, event | category | flops | bytes accessed | tf_op | source)
XLA Modules:
  0.0 72.4 jit_solution(6185375689266627679)
XLA Ops:
  0.6 3.6 %left.1 = (bf16[2,2,1024,512]{3,2,1,0:T(8,128)(2,1)S(1)}, f32[1024,512]{1,0:T(8,128)S(1)}, f32[8,32,128]{2,1,0:T(8,128)S(1)}, f32[8,32,128]{2,1,0:T(8,128)S(1)}) custom-call(bf16[2,1024,512]{2,1,0:T(8,128)(2,1)} %bitcast.10, f32[2,1024,512]{2,1,0:T(8,128)} %bitcast.9, f32[2,32,512]{2,1,0:T(8,128)} %bitcast.11), custom_call_target="tpu_custom_call" | custom-call | tf_op jit(solution)/shard_map/left/pallas_call | solution.py:98
  4.3 3.3 %collective-permute-start = (f32[8,32,128]{2,1,0:T(8,128)S(1)}, f32[8,32,128]{2,1,0:T(8,128)S(1)}, u32[]{:S(2)}, u32[]{:S(2)}) collective-permute-start(f32[8,32,128]{2,1,0:T(8,128)S(1)} %get-tuple-element.21), channel_id=1, source_target_pairs={{0,8},{8,0},{16,24},{24,16},{32,40},{40,32},{48,56},{56,48},{64,72... | collective-permute-start | bytes 393224 | tf_op jit(solution)/shard_map/ppermute | solution.py:339
  7.6 1.0 %collective-permute-done.refs_1_ = f32[8,32,128]{2,1,0:T(8,128)S(1)} collective-permute-done((f32[8,32,128]{2,1,0:T(8,128)S(1)}, f32[8,32,128]{2,1,0:T(8,128)S(1)}, u32[]{:S(2)}, u32[]{:S(2)}) %collective-permute-start) | collective-permute-done | bytes 131104 | tf_op jit(solution)/shard_map/ppermute | solution.py:339
  8.6 0.4 collective-permute-start.1
  9.1 1.2 %collective-permute-start.4 = (f32[8,32,128]{2,1,0:T(8,128)S(1)}, f32[8,32,128]{2,1,0:T(8,128)S(1)}, u32[]{:S(2)}, u32[]{:S(2)}) collective-permute-start(f32[8,32,128]{2,1,0:T(8,128)S(1)} %add.3.refs_0_), channel_id=1, source_target_pairs={{0,128},{8,40},{16,144},{24,56},{32,160},{40,8},{48,176},{56,24},{... | collective-permute-start | bytes 393224 | tf_op jit(solution)/shard_map/ppermute | solution.py:339
  10.2 0.8 %collective-permute-start.3 = (f32[8,32,128]{2,1,0:T(8,128)S(1)}, f32[8,32,128]{2,1,0:T(8,128)S(1)}, u32[]{:S(2)}, u32[]{:S(2)}) collective-permute-start(f32[8,32,128]{2,1,0:T(8,128)S(1)} %add.3.refs_0_), channel_id=1, source_target_pairs={{0,192},{8,56},{16,208},{24,40},{32,224},{40,24},{48,240},{56,8},{... | collective-permute-start | bytes 393224 | tf_op jit(solution)/shard_map/ppermute | solution.py:339
  11.0 0.7 collective-permute-start.2
  11.7 3.0 %collective-permute-done.4.refs_3_ = f32[8,32,128]{2,1,0:T(8,128)S(1)} collective-permute-done((f32[8,32,128]{2,1,0:T(8,128)S(1)}, f32[8,32,128]{2,1,0:T(8,128)S(1)}, u32[]{:S(2)}, u32[]{:S(2)}) %collective-permute-start.4) | collective-permute-done | bytes 131104 | tf_op jit(solution)/shard_map/ppermute | solution.py:339
  14.7 1.4 %collective-permute-done.3.refs_2_ = f32[8,32,128]{2,1,0:T(8,128)S(1)} collective-permute-done((f32[8,32,128]{2,1,0:T(8,128)S(1)}, f32[8,32,128]{2,1,0:T(8,128)S(1)}, u32[]{:S(2)}, u32[]{:S(2)}) %collective-permute-start.3) | collective-permute-done | bytes 131104 | tf_op jit(solution)/shard_map/ppermute | solution.py:339
  16.1 0.0 collective-permute-done.2.refs_1_
  16.1 2.0 %collective-permute-start.7 = (f32[8,32,128]{2,1,0:T(8,128)S(1)}, f32[8,32,128]{2,1,0:T(8,128)S(1)}, u32[]{:S(2)}, u32[]{:S(2)}) collective-permute-start(f32[8,32,128]{2,1,0:T(8,128)S(1)} %add.4.refs_0_), channel_id=1, source_target_pairs={{0,32},{8,136},{16,48},{24,152},{32,0},{40,168},{48,16},{56,184},{... | collective-permute-start | bytes 393224 | tf_op jit(solution)/shard_map/ppermute | solution.py:339
  18.1 0.9 %collective-permute-start.6 = (f32[8,32,128]{2,1,0:T(8,128)S(1)}, f32[8,32,128]{2,1,0:T(8,128)S(1)}, u32[]{:S(2)}, u32[]{:S(2)}) collective-permute-start(f32[8,32,128]{2,1,0:T(8,128)S(1)} %add.4.refs_0_), channel_id=1, source_target_pairs={{0,48},{8,200},{16,32},{24,216},{32,16},{40,232},{48,0},{56,248},{... | collective-permute-start | bytes 393224 | tf_op jit(solution)/shard_map/ppermute | solution.py:339
  19.0 0.0 collective-permute-start.5
  19.0 2.5 %collective-permute-done.7.refs_3_ = f32[8,32,128]{2,1,0:T(8,128)S(1)} collective-permute-done((f32[8,32,128]{2,1,0:T(8,128)S(1)}, f32[8,32,128]{2,1,0:T(8,128)S(1)}, u32[]{:S(2)}, u32[]{:S(2)}) %collective-permute-start.7) | collective-permute-done | bytes 131104 | tf_op jit(solution)/shard_map/ppermute | solution.py:339
  21.5 1.8 %collective-permute-done.6.refs_2_ = f32[8,32,128]{2,1,0:T(8,128)S(1)} collective-permute-done((f32[8,32,128]{2,1,0:T(8,128)S(1)}, f32[8,32,128]{2,1,0:T(8,128)S(1)}, u32[]{:S(2)}, u32[]{:S(2)}) %collective-permute-start.6) | collective-permute-done | bytes 131104 | tf_op jit(solution)/shard_map/ppermute | solution.py:339
  23.3 3.0 %collective-permute-start.8 = (f32[8,32,128]{2,1,0:T(8,128)S(1)}, f32[8,32,128]{2,1,0:T(8,128)S(1)}, u32[]{:S(2)}, u32[]{:S(2)}) collective-permute-start(f32[8,32,128]{2,1,0:T(8,128)S(1)} %add.5.p_t), channel_id=1, source_target_pairs={{0,8},{8,0},{16,24},{24,16},{32,40},{40,32},{48,56},{56,48},{64,72... | collective-permute-start | bytes 393224 | tf_op jit(solution)/shard_map/ppermute | solution.py:339
  26.3 0.5 pair.1.pair_terms
  26.8 0.6 right.1
  27.5 10.9 %all_to_all.15.raw = f32[16,8,128]{2,1,0:T(8,128)S(1)} all-to-all(f32[16,8,128]{2,1,0:T(8,128)S(1)} %bitcast.8), channel_id=1, replica_groups={{0,16,32,48,64,80,96,112,128,144,160,176,192,208,224,240},{8,24,40,56,7..., dimensions={0} | all-to-all | bytes 131072 | tf_op jit(solution)/shard_map/all_to_all | solution.py:330
  38.4 0.3 mix.1
  38.7 15.7 %all_to_all.16.x = f32[8,24,128]{2,1,0:T(8,128)S(1)} all-to-all(f32[8,24,128]{2,1,0:T(8,128)S(1)} %mix.1), channel_id=1, replica_groups=mesh['dp'=32,'tensor'=8] {'tensor'}, dimensions={0} | all-to-all | bytes 196608 | tf_op jit(solution)/shard_map/all_to_all | solution.py:330
  54.3 0.7 %unmix.1 = (f32[32,8,128]{2,1,0:T(8,128)S(1)}, f32[2,32,32]{2,1,0:T(8,128)S(1)}) custom-call(f32[8,24,128]{2,1,0:T(8,128)S(1)} %all_to_all.16.x), custom_call_target="tpu_custom_call" | custom-call | tf_op jit(solution)/shard_map/unmix/pallas_call | solution.py:251
  55.1 13.9 %all_to_all.17.raw = f32[32,8,128]{2,1,0:T(8,128)S(1)} all-to-all(f32[32,8,128]{2,1,0:T(8,128)S(1)} %get-tuple-element.31), channel_id=1, replica_groups=mesh['dp'=32,'tensor'=8] {'dp'}, dimensions={0} | all-to-all | bytes 262144 | tf_op jit(solution)/shard_map/all_to_all | solution.py:330
  69.0 3.4 %last.1 = (bf16[2,1024,512]{2,1,0:T(8,128)(2,1)}, f32[2,1024,512]{2,1,0:T(8,128)}, f32[2,32,512]{2,1,0:T(8,128)}) custom-call(bf16[2,2,1024,512]{3,2,1,0:T(8,128)(2,1)S(1)} %get-tuple-element.19.terms, bf16[1024,128]{1,0:T(8,128)(2,1)S(1)} %get-tuple-element.25.p_terms, f32[8,32,128]{2,1,0:T(8,128)S(1)} %collective-permute-done.8.p_other, ...), custom_call_target="tpu_custom_call" | custom-call | tf_op jit(solution)/shard_map/last/pallas_call | solution.py:307
  (6 shorter events, 0.1 us)
Async XLA Ops:
  4.3 4.3 %collective-permute-start = (f32[8,32,128]{2,1,0:T(8,128)S(1)}, f32[8,32,128]{2,1,0:T(8,128)S(1)}, u32[]{:S(2)}, u32[]{:S(2)}) collective-permute-start(f32[8,32,128]{2,1,0:T(8,128)S(1)} %get-tuple-element.21), channel_id=1, source_target_pairs={{0,8},{8,0},{16,24},{24,16},{32,40},{40,32},{48,56},{56,48},{64,72... | collective-permute-start | bytes 393224 | tf_op jit(solution)/shard_map/ppermute | solution.py:339
  8.6 17.7 %collective-permute-start.1 = (f32[1024,512]{1,0:T(8,128)S(1)}, f32[1024,512]{1,0:T(8,128)S(1)}, u32[]{:S(2)}, u32[]{:S(2)}) collective-permute-start(f32[1024,512]{1,0:T(8,128)S(1)} %get-tuple-element.23), channel_id=1, source_target_pairs={{0,8},{8,0},{16,24},{24,16},{32,40},{40,32},{48,56},{56,48},{64,72... | collective-permute-start | bytes 6291464 | tf_op jit(solution)/shard_map/ppermute | solution.py:339
  9.1 5.6 %collective-permute-start.4 = (f32[8,32,128]{2,1,0:T(8,128)S(1)}, f32[8,32,128]{2,1,0:T(8,128)S(1)}, u32[]{:S(2)}, u32[]{:S(2)}) collective-permute-start(f32[8,32,128]{2,1,0:T(8,128)S(1)} %add.3.refs_0_), channel_id=1, source_target_pairs={{0,128},{8,40},{16,144},{24,56},{32,160},{40,8},{48,176},{56,24},{... | collective-permute-start | bytes 393224 | tf_op jit(solution)/shard_map/ppermute | solution.py:339
  10.2 5.8 %collective-permute-start.3 = (f32[8,32,128]{2,1,0:T(8,128)S(1)}, f32[8,32,128]{2,1,0:T(8,128)S(1)}, u32[]{:S(2)}, u32[]{:S(2)}) collective-permute-start(f32[8,32,128]{2,1,0:T(8,128)S(1)} %add.3.refs_0_), channel_id=1, source_target_pairs={{0,192},{8,56},{16,208},{24,40},{32,224},{40,24},{48,240},{56,8},{... | collective-permute-start | bytes 393224 | tf_op jit(solution)/shard_map/ppermute | solution.py:339
  11.0 5.1 %collective-permute-start.2 = (f32[8,32,128]{2,1,0:T(8,128)S(1)}, f32[8,32,128]{2,1,0:T(8,128)S(1)}, u32[]{:S(2)}, u32[]{:S(2)}) collective-permute-start(f32[8,32,128]{2,1,0:T(8,128)S(1)} %add.3.refs_0_), channel_id=1, source_target_pairs={{0,64},{8,24},{16,80},{24,8},{32,96},{40,56},{48,112},{56,40},{64,... | collective-permute-start | bytes 393224 | tf_op jit(solution)/shard_map/ppermute | solution.py:339
  16.1 5.4 %collective-permute-start.7 = (f32[8,32,128]{2,1,0:T(8,128)S(1)}, f32[8,32,128]{2,1,0:T(8,128)S(1)}, u32[]{:S(2)}, u32[]{:S(2)}) collective-permute-start(f32[8,32,128]{2,1,0:T(8,128)S(1)} %add.4.refs_0_), channel_id=1, source_target_pairs={{0,32},{8,136},{16,48},{24,152},{32,0},{40,168},{48,16},{56,184},{... | collective-permute-start | bytes 393224 | tf_op jit(solution)/shard_map/ppermute | solution.py:339
  18.1 5.1 %collective-permute-start.6 = (f32[8,32,128]{2,1,0:T(8,128)S(1)}, f32[8,32,128]{2,1,0:T(8,128)S(1)}, u32[]{:S(2)}, u32[]{:S(2)}) collective-permute-start(f32[8,32,128]{2,1,0:T(8,128)S(1)} %add.4.refs_0_), channel_id=1, source_target_pairs={{0,48},{8,200},{16,32},{24,216},{32,16},{40,232},{48,0},{56,248},{... | collective-permute-start | bytes 393224 | tf_op jit(solution)/shard_map/ppermute | solution.py:339
  19.0 4.3 %collective-permute-start.5 = (f32[8,32,128]{2,1,0:T(8,128)S(1)}, f32[8,32,128]{2,1,0:T(8,128)S(1)}, u32[]{:S(2)}, u32[]{:S(2)}) collective-permute-start(f32[8,32,128]{2,1,0:T(8,128)S(1)} %add.4.refs_0_), channel_id=1, source_target_pairs={{0,16},{8,72},{16,0},{24,88},{32,48},{40,104},{48,32},{56,120},{64... | collective-permute-start | bytes 393224 | tf_op jit(solution)/shard_map/ppermute | solution.py:339
  23.3 4.1 %collective-permute-start.8 = (f32[8,32,128]{2,1,0:T(8,128)S(1)}, f32[8,32,128]{2,1,0:T(8,128)S(1)}, u32[]{:S(2)}, u32[]{:S(2)}) collective-permute-start(f32[8,32,128]{2,1,0:T(8,128)S(1)} %add.5.p_t), channel_id=1, source_target_pairs={{0,8},{8,0},{16,24},{24,16},{32,40},{40,32},{48,56},{56,48},{64,72... | collective-permute-start | bytes 393224 | tf_op jit(solution)/shard_map/ppermute | solution.py:339

commit v7 on v6

--- a/solution.py
+++ b/solution.py
@@ -158,20 +158,31 @@
     return jnp.concatenate([one, two, one, jnp.zeros_like(one)], 0).T
 
 
-def packed_gram(factor):
-    rank = factor.shape[0]
-    square = dot(factor, factor, ((1,), (1,)), highest)
-    return jnp.concatenate([square[at : at + 8] for at in range(0, rank, 8)], 1)
-
-
-def right_kernel(pair_terms, p_t, raw, gram, p_terms):
+def gram_of(p_t):
+    tiles, rank, _ = p_t.shape
+
+    def kernel(p_t, out):
+        factor = jnp.concatenate([p_t[at] for at in range(tiles)], 1)
+        square = dot(factor, factor, ((1,), (1,)), highest)
+        out[...] = jnp.concatenate([square[at : at + 8] for at in range(0, rank, 8)], 1)
+
+    return pl.pallas_call(
+        kernel,
+        in_specs=[whole],
+        out_specs=whole,
+        out_shape=pltpu.VMEM((8, 128), f32),
+        compiler_params=params,
+        name="gram",
+    )(in_vmem(p_t))
+
+
+def right_kernel(pair_terms, p_t, raw, p_terms):
     tiles, rank, _ = p_t.shape
     factor = jnp.concatenate([p_t[at] for at in range(tiles)], 1)
     small = thirds(factor)
     term = split_dot(small, pair_terms[0], pair_terms[1], ((1,), (0,)))
     for at in range(raw.shape[0]):
         raw[at] = term[:, at * 128 : (at + 1) * 128]
-    gram[...] = packed_gram(factor)
     p_terms[...] = stack_terms(*small[:2])
 
 
@@ -181,10 +192,9 @@
     return pl.pallas_call(
         right_kernel,
         in_specs=[whole] * 2,
-        out_specs=[whole] * 3,
+        out_specs=[whole] * 2,
         out_shape=[
             pltpu.VMEM((cols // 128, rank, 128), f32),
-            pltpu.VMEM((8, 128), f32),
             pltpu.VMEM((rows, 4 * rank), bf16),
         ],
         compiler_params=params,
@@ -192,10 +202,9 @@
     )(in_vmem(pair_terms), in_vmem(p_t))
 
 
-def mix(raw, gram, p_other, copies):
-    def kernel(raw, gram, p_other, out):
-        factor = jnp.concatenate([p_other[at] for at in range(p_other.shape[0])], 1)
-        both = jnp.concatenate([jnp.sum(raw[...], axis=0), gram[...], packed_gram(factor)], 0)
+def mix(raw, gram, gram_other, copies):
+    def kernel(raw, gram, gram_other, out):
+        both = jnp.concatenate([jnp.sum(raw[...], axis=0), gram[...], gram_other[...]], 0)
         out[...] = jnp.broadcast_to(both[None], out.shape)
 
     return pl.pallas_call(
@@ -205,7 +214,7 @@
         out_shape=pltpu.VMEM((copies, 24, 128), f32),
         compiler_params=params,
         name="mix",
-    )(in_vmem(raw), in_vmem(gram), in_vmem(p_other))
+    )(in_vmem(raw), in_vmem(gram), in_vmem(gram_other))
 
 
 def lower_inverses(packed, rank):
@@ -357,11 +366,12 @@
     total, merged = lax.optimization_barrier((add([own, swap_cores(other)]), merged))
     pair_terms = pair(terms, swap_cores(merged))
     p_t = sum_axis(sum_axis(total, 0, 1.0), 1, 1.0 / replicas)
-    raw, gram, p_terms = right(pair_terms, p_t)
-    raw, p_other = lax.optimization_barrier((raw, swap_cores(p_t)))
+    gram = gram_of(p_t)
+    raw, p_terms = right(pair_terms, p_t)
+    raw, p_other, gram_other = lax.optimization_barrier((raw, swap_cores(p_t), swap_cores(gram)))
     chips = [[2 * chip + core for chip in range(replicas // 2)] for core in range(2)]
     raw = exchange(raw.reshape(replicas // 2, 8, 128), "dp", chips)
-    both = exchange(mix(raw, gram, p_other, slabs), "tensor")
+    both = exchange(mix(raw, gram, gram_other, slabs), "tensor")
     raw, inverse = unmix(both, replicas, rank, 1.0 / replicas)
     decompressed, new_errors, q_new = last(terms, p_terms, p_other, inverse, exchange(raw, "dp"))
     return decompressed, new_errors[:, None], jnp.swapaxes(q_new, 1, 2)

time: 72.6 us -> 72.8 us (level)
    ppermute x9 -> x10, waiting for transfers between devices: 9.65 us -> 9.8 us  [swap(): return lax.ppermute(x, 'dp', pairs)]
    ppermute x9 -> x10, starting transfers between devices: 12.3 us -> 12.3 us  [swap(): return lax.ppermute(x, 'dp', pairs)]
  transfers between devices with their start and end apart: 9 -> 10, of which waited for: 5 -> 6; matrix products, arithmetic and copies ran while one was open for 0% -> 0% of each run, Pallas kernels for 2% -> 2%
where the time goes in v7:
time: 72.8 us; the launch traced here: 72.6 us
  blocking collectives  40.6 us (56%)
  starting transfers between devices  12.3 us (17%)
  waiting for transfers between devices  9.8 us (13%)
  Pallas kernels  9.18 us (13%)
    all_to_all x3, blocking collectives, exchange(): return lax.all_to_all(x, axis, 0, 0, axis_index_groups=groups, tiled=True)  40.6 us
    ppermute x10, starting transfers between devices, swap(): return lax.ppermute(x, 'dp', pairs)  12.3 us
    ppermute x10, waiting for transfers between devices, swap(): return lax.ppermute(x, 'dp', pairs)  9.8 us
    pallas_call x1, Pallas kernels, left(): pl.pallas_call(left_kernel, in_specs=[pl.BlockSpec(memory_space=pltpu.HBM...  3.64 us
    pallas_call x1, Pallas kernels, last(): pl.pallas_call(last_kernel, in_specs=[whole] * 5, out_specs=[pl.BlockSpec...  3.42 us
  transfers between devices with their start and end apart: 10, of which 6 were waited for; matrix products, arithmetic and copies ran while one was open for 0% of the time, Pallas kernels for 2%

profile of v7, /device:TPU:1, one launch (start us, length us, event | category | flops | bytes accessed | tf_op | source)
XLA Modules:
  0.0 72.6 jit_solution(14276911353793925594)
XLA Ops:
  0.6 3.6 %left.1 = (bf16[2,2,1024,512]{3,2,1,0:T(8,128)(2,1)S(1)}, f32[1024,512]{1,0:T(8,128)S(1)}, f32[8,32,128]{2,1,0:T(8,128)S(1)}, f32[8,32,128]{2,1,0:T(8,128)S(1)}) custom-call(bf16[2,1024,512]{2,1,0:T(8,128)(2,1)} %bitcast.10, f32[2,1024,512]{2,1,0:T(8,128)} %bitcast.9, f32[2,32,512]{2,1,0:T(8,128)} %bitcast.11), custom_call_target="tpu_custom_call" | custom-call | tf_op jit(solution)/shard_map/left/pallas_call | solution.py:98
  4.3 3.3 %collective-permute-start = (f32[8,32,128]{2,1,0:T(8,128)S(1)}, f32[8,32,128]{2,1,0:T(8,128)S(1)}, u32[]{:S(2)}, u32[]{:S(2)}) collective-permute-start(f32[8,32,128]{2,1,0:T(8,128)S(1)} %get-tuple-element.21), channel_id=1, source_target_pairs={{0,8},{8,0},{16,24},{24,16},{32,40},{40,32},{48,56},{56,48},{64,72... | collective-permute-start | bytes 393224 | tf_op jit(solution)/shard_map/ppermute | solution.py:348
  7.6 1.0 %collective-permute-done.refs_1_ = f32[8,32,128]{2,1,0:T(8,128)S(1)} collective-permute-done((f32[8,32,128]{2,1,0:T(8,128)S(1)}, f32[8,32,128]{2,1,0:T(8,128)S(1)}, u32[]{:S(2)}, u32[]{:S(2)}) %collective-permute-start) | collective-permute-done | bytes 131104 | tf_op jit(solution)/shard_map/ppermute | solution.py:348
  8.6 0.4 collective-permute-start.1
  9.1 1.2 %collective-permute-start.4 = (f32[8,32,128]{2,1,0:T(8,128)S(1)}, f32[8,32,128]{2,1,0:T(8,128)S(1)}, u32[]{:S(2)}, u32[]{:S(2)}) collective-permute-start(f32[8,32,128]{2,1,0:T(8,128)S(1)} %add.3.refs_0_), channel_id=1, source_target_pairs={{0,128},{8,40},{16,144},{24,56},{32,160},{40,8},{48,176},{56,24},{... | collective-permute-start | bytes 393224 | tf_op jit(solution)/shard_map/ppermute | solution.py:348
  10.2 0.8 %collective-permute-start.3 = (f32[8,32,128]{2,1,0:T(8,128)S(1)}, f32[8,32,128]{2,1,0:T(8,128)S(1)}, u32[]{:S(2)}, u32[]{:S(2)}) collective-permute-start(f32[8,32,128]{2,1,0:T(8,128)S(1)} %add.3.refs_0_), channel_id=1, source_target_pairs={{0,192},{8,56},{16,208},{24,40},{32,224},{40,24},{48,240},{56,8},{... | collective-permute-start | bytes 393224 | tf_op jit(solution)/shard_map/ppermute | solution.py:348
  11.0 0.7 collective-permute-start.2
  11.7 3.0 %collective-permute-done.4.refs_3_ = f32[8,32,128]{2,1,0:T(8,128)S(1)} collective-permute-done((f32[8,32,128]{2,1,0:T(8,128)S(1)}, f32[8,32,128]{2,1,0:T(8,128)S(1)}, u32[]{:S(2)}, u32[]{:S(2)}) %collective-permute-start.4) | collective-permute-done | bytes 131104 | tf_op jit(solution)/shard_map/ppermute | solution.py:348
  14.7 1.4 %collective-permute-done.3.refs_2_ = f32[8,32,128]{2,1,0:T(8,128)S(1)} collective-permute-done((f32[8,32,128]{2,1,0:T(8,128)S(1)}, f32[8,32,128]{2,1,0:T(8,128)S(1)}, u32[]{:S(2)}, u32[]{:S(2)}) %collective-permute-start.3) | collective-permute-done | bytes 131104 | tf_op jit(solution)/shard_map/ppermute | solution.py:348
  16.1 2.0 %collective-permute-start.7 = (f32[8,32,128]{2,1,0:T(8,128)S(1)}, f32[8,32,128]{2,1,0:T(8,128)S(1)}, u32[]{:S(2)}, u32[]{:S(2)}) collective-permute-start(f32[8,32,128]{2,1,0:T(8,128)S(1)} %add.4.refs_0_), channel_id=1, source_target_pairs={{0,32},{8,136},{16,48},{24,152},{32,0},{40,168},{48,16},{56,184},{... | collective-permute-start | bytes 393224 | tf_op jit(solution)/shard_map/ppermute | solution.py:348
  18.1 0.9 %collective-permute-start.6 = (f32[8,32,128]{2,1,0:T(8,128)S(1)}, f32[8,32,128]{2,1,0:T(8,128)S(1)}, u32[]{:S(2)}, u32[]{:S(2)}) collective-permute-start(f32[8,32,128]{2,1,0:T(8,128)S(1)} %add.4.refs_0_), channel_id=1, source_target_pairs={{0,48},{8,200},{16,32},{24,216},{32,16},{40,232},{48,0},{56,248},{... | collective-permute-start | bytes 393224 | tf_op jit(solution)/shard_map/ppermute | solution.py:348
  19.0 2.5 %collective-permute-done.7.refs_3_ = f32[8,32,128]{2,1,0:T(8,128)S(1)} collective-permute-done((f32[8,32,128]{2,1,0:T(8,128)S(1)}, f32[8,32,128]{2,1,0:T(8,128)S(1)}, u32[]{:S(2)}, u32[]{:S(2)}) %collective-permute-start.7) | collective-permute-done | bytes 131104 | tf_op jit(solution)/shard_map/ppermute | solution.py:348
  21.5 1.8 %collective-permute-done.6.refs_2_ = f32[8,32,128]{2,1,0:T(8,128)S(1)} collective-permute-done((f32[8,32,128]{2,1,0:T(8,128)S(1)}, f32[8,32,128]{2,1,0:T(8,128)S(1)}, u32[]{:S(2)}, u32[]{:S(2)}) %collective-permute-start.6) | collective-permute-done | bytes 131104 | tf_op jit(solution)/shard_map/ppermute | solution.py:348
  23.3 3.0 %collective-permute-start.8 = (f32[8,32,128]{2,1,0:T(8,128)S(1)}, f32[8,32,128]{2,1,0:T(8,128)S(1)}, u32[]{:S(2)}, u32[]{:S(2)}) collective-permute-start(f32[8,32,128]{2,1,0:T(8,128)S(1)} %add.5.p_t), channel_id=1, source_target_pairs={{0,8},{8,0},{16,24},{24,16},{32,40},{40,32},{48,56},{56,48},{64,72... | collective-permute-start | bytes 393224 | tf_op jit(solution)/shard_map/ppermute | solution.py:348
  26.3 0.3 gram.1
  26.6 0.0 collective-permute-start.9
  26.7 0.5 pair.1.pair_terms
  27.2 0.5 right.1
  27.7 0.1 collective-permute-done.9.gram_other
  27.8 10.9 %all_to_all.15.raw = f32[16,8,128]{2,1,0:T(8,128)S(1)} all-to-all(f32[16,8,128]{2,1,0:T(8,128)S(1)} %bitcast.8), channel_id=1, replica_groups={{0,16,32,48,64,80,96,112,128,144,160,176,192,208,224,240},{8,24,40,56,7..., dimensions={0} | all-to-all | bytes 131072 | tf_op jit(solution)/shard_map/all_to_all | solution.py:339
  38.7 15.7 %all_to_all.16.x = f32[8,24,128]{2,1,0:T(8,128)S(1)} all-to-all(f32[8,24,128]{2,1,0:T(8,128)S(1)} %mix.1), channel_id=1, replica_groups=mesh['dp'=32,'tensor'=8] {'tensor'}, dimensions={0} | all-to-all | bytes 196608 | tf_op jit(solution)/shard_map/all_to_all | solution.py:339
  54.4 0.7 %unmix.1 = (f32[32,8,128]{2,1,0:T(8,128)S(1)}, f32[2,32,32]{2,1,0:T(8,128)S(1)}) custom-call(f32[8,24,128]{2,1,0:T(8,128)S(1)} %all_to_all.16.x), custom_call_target="tpu_custom_call" | custom-call | tf_op jit(solution)/shard_map/unmix/pallas_call | solution.py:260
  55.1 14.1 %all_to_all.17.raw = f32[32,8,128]{2,1,0:T(8,128)S(1)} all-to-all(f32[32,8,128]{2,1,0:T(8,128)S(1)} %get-tuple-element.31), channel_id=1, replica_groups=mesh['dp'=32,'tensor'=8] {'dp'}, dimensions={0} | all-to-all | bytes 262144 | tf_op jit(solution)/shard_map/all_to_all | solution.py:339
  69.2 3.4 %last.1 = (bf16[2,1024,512]{2,1,0:T(8,128)(2,1)}, f32[2,1024,512]{2,1,0:T(8,128)}, f32[2,32,512]{2,1,0:T(8,128)}) custom-call(bf16[2,2,1024,512]{3,2,1,0:T(8,128)(2,1)S(1)} %get-tuple-element.19.terms, bf16[1024,128]{1,0:T(8,128)(2,1)S(1)} %get-tuple-element.25.p_terms, f32[8,32,128]{2,1,0:T(8,128)S(1)} %collective-permute-done.8.p_other, ...), custom_call_target="tpu_custom_call" | custom-call | tf_op jit(solution)/shard_map/last/pallas_call | solution.py:316
  (9 shorter events, 0.1 us)
Async XLA Ops:
  4.3 4.3 %collective-permute-start = (f32[8,32,128]{2,1,0:T(8,128)S(1)}, f32[8,32,128]{2,1,0:T(8,128)S(1)}, u32[]{:S(2)}, u32[]{:S(2)}) collective-permute-start(f32[8,32,128]{2,1,0:T(8,128)S(1)} %get-tuple-element.21), channel_id=1, source_target_pairs={{0,8},{8,0},{16,24},{24,16},{32,40},{40,32},{48,56},{56,48},{64,72... | collective-permute-start | bytes 393224 | tf_op jit(solution)/shard_map/ppermute | solution.py:348
  8.6 18.0 %collective-permute-start.1 = (f32[1024,512]{1,0:T(8,128)S(1)}, f32[1024,512]{1,0:T(8,128)S(1)}, u32[]{:S(2)}, u32[]{:S(2)}) collective-permute-start(f32[1024,512]{1,0:T(8,128)S(1)} %get-tuple-element.23), channel_id=1, source_target_pairs={{0,8},{8,0},{16,24},{24,16},{32,40},{40,32},{48,56},{56,48},{64,72... | collective-permute-start | bytes 6291464 | tf_op jit(solution)/shard_map/ppermute | solution.py:348
  9.1 5.6 %collective-permute-start.4 = (f32[8,32,128]{2,1,0:T(8,128)S(1)}, f32[8,32,128]{2,1,0:T(8,128)S(1)}, u32[]{:S(2)}, u32[]{:S(2)}) collective-permute-start(f32[8,32,128]{2,1,0:T(8,128)S(1)} %add.3.refs_0_), channel_id=1, source_target_pairs={{0,128},{8,40},{16,144},{24,56},{32,160},{40,8},{48,176},{56,24},{... | collective-permute-start | bytes 393224 | tf_op jit(solution)/shard_map/ppermute | solution.py:348
  10.2 5.8 %collective-permute-start.3 = (f32[8,32,128]{2,1,0:T(8,128)S(1)}, f32[8,32,128]{2,1,0:T(8,128)S(1)}, u32[]{:S(2)}, u32[]{:S(2)}) collective-permute-start(f32[8,32,128]{2,1,0:T(8,128)S(1)} %add.3.refs_0_), channel_id=1, source_target_pairs={{0,192},{8,56},{16,208},{24,40},{32,224},{40,24},{48,240},{56,8},{... | collective-permute-start | bytes 393224 | tf_op jit(solution)/shard_map/ppermute | solution.py:348
  11.0 5.1 %collective-permute-start.2 = (f32[8,32,128]{2,1,0:T(8,128)S(1)}, f32[8,32,128]{2,1,0:T(8,128)S(1)}, u32[]{:S(2)}, u32[]{:S(2)}) collective-permute-start(f32[8,32,128]{2,1,0:T(8,128)S(1)} %add.3.refs_0_), channel_id=1, source_target_pairs={{0,64},{8,24},{16,80},{24,8},{32,96},{40,56},{48,112},{56,40},{64,... | collective-permute-start | bytes 393224 | tf_op jit(solution)/shard_map/ppermute | solution.py:348
  16.1 5.4 %collective-permute-start.7 = (f32[8,32,128]{2,1,0:T(8,128)S(1)}, f32[8,32,128]{2,1,0:T(8,128)S(1)}, u32[]{:S(2)}, u32[]{:S(2)}) collective-permute-start(f32[8,32,128]{2,1,0:T(8,128)S(1)} %add.4.refs_0_), channel_id=1, source_target_pairs={{0,32},{8,136},{16,48},{24,152},{32,0},{40,168},{48,16},{56,184},{... | collective-permute-start | bytes 393224 | tf_op jit(solution)/shard_map/ppermute | solution.py:348
  18.1 5.1 %collective-permute-start.6 = (f32[8,32,128]{2,1,0:T(8,128)S(1)}, f32[8,32,128]{2,1,0:T(8,128)S(1)}, u32[]{:S(2)}, u32[]{:S(2)}) collective-permute-start(f32[8,32,128]{2,1,0:T(8,128)S(1)} %add.4.refs_0_), channel_id=1, source_target_pairs={{0,48},{8,200},{16,32},{24,216},{32,16},{40,232},{48,0},{56,248},{... | collective-permute-start | bytes 393224 | tf_op jit(solution)/shard_map/ppermute | solution.py:348
  19.0 4.3 %collective-permute-start.5 = (f32[8,32,128]{2,1,0:T(8,128)S(1)}, f32[8,32,128]{2,1,0:T(8,128)S(1)}, u32[]{:S(2)}, u32[]{:S(2)}) collective-permute-start(f32[8,32,128]{2,1,0:T(8,128)S(1)} %add.4.refs_0_), channel_id=1, source_target_pairs={{0,16},{8,72},{16,0},{24,88},{32,48},{40,104},{48,32},{56,120},{64... | collective-permute-start | bytes 393224 | tf_op jit(solution)/shard_map/ppermute | solution.py:348
  23.3 4.5 %collective-permute-start.8 = (f32[8,32,128]{2,1,0:T(8,128)S(1)}, f32[8,32,128]{2,1,0:T(8,128)S(1)}, u32[]{:S(2)}, u32[]{:S(2)}) collective-permute-start(f32[8,32,128]{2,1,0:T(8,128)S(1)} %add.5.p_t), channel_id=1, source_target_pairs={{0,8},{8,0},{16,24},{24,16},{32,40},{40,32},{48,56},{56,48},{64,72... | collective-permute-start | bytes 393224 | tf_op jit(solution)/shard_map/ppermute | solution.py:348
  26.6 1.2 %collective-permute-start.9 = (f32[8,128]{1,0:T(8,128)S(1)}, f32[8,128]{1,0:T(8,128)S(1)}, u32[]{:S(2)}, u32[]{:S(2)}) collective-permute-start(f32[8,128]{1,0:T(8,128)S(1)} %gram.1), channel_id=1, source_target_pairs={{0,8},{8,0},{16,24},{24,16},{32,40},{40,32},{48,56},{56,48},{64,72... | collective-permute-start | bytes 12296 | tf_op jit(solution)/shard_map/ppermute | solution.py:348

commit v8 on v6

--- a/solution.py
+++ b/solution.py
@@ -67,11 +67,11 @@
         )
 
     q_copy = pltpu.make_async_copy(q_t, q_here, q_sem)
-    q_copy.start()
     for n in range(ahead):
         for copy in fetch(n):
             copy.start()
-    q_copy.wait()
+        if n == 0:
+            q_copy.start()
     for n, (l, b) in enumerate(pieces):
         for copy in fetch(n):
             copy.wait()
@@ -85,6 +85,8 @@
         merged_high, merged_low = halves(merged)
         terms[l, 0, at] = merged_high
         terms[l, 1, at] = merged_low
+        if n == 0:
+            q_copy.wait()
         term = split_dot(thirds(q_here[l]), merged_high, merged_low, ((1,), (1,)))
         part = other if n < len(pieces) // 2 else own
         for lane in range(block_rows // 128):

time: 72.6 us -> 72.7 us (level)
  no operation moved by 1% of the time
where the time goes in v8:
time: 72.7 us; the launch traced here: 72.5 us
  blocking collectives  40.4 us (56%)
  starting transfers between devices  12.3 us (17%)
  waiting for transfers between devices  9.66 us (13%)
  Pallas kernels  9.45 us (13%)
    all_to_all x3, blocking collectives, exchange(): return lax.all_to_all(x, axis, 0, 0, axis_index_groups=groups, tiled=True)  40.4 us
    ppermute x9, starting transfers between devices, swap(): return lax.ppermute(x, 'dp', pairs)  12.3 us
    ppermute x9, waiting for transfers between devices, swap(): return lax.ppermute(x, 'dp', pairs)  9.66 us
    pallas_call x1, Pallas kernels, left(): pl.pallas_call(left_kernel, in_specs=[pl.BlockSpec(memory_space=pltpu.HBM...  3.76 us
    pallas_call x1, Pallas kernels, last(): pl.pallas_call(last_kernel, in_specs=[whole] * 5, out_specs=[pl.BlockSpec...  3.42 us
  transfers between devices with their start and end apart: 9, of which 5 were waited for; matrix products, arithmetic and copies ran while one was open for 0% of the time, Pallas kernels for 2%

profile of v8, /device:TPU:1, one launch (start us, length us, event | category | flops | bytes accessed | tf_op | source)
XLA Modules:
  0.0 72.5 jit_solution(6167645215027709268)
XLA Ops:
  0.6 3.8 %left.1 = (bf16[2,2,1024,512]{3,2,1,0:T(8,128)(2,1)S(1)}, f32[1024,512]{1,0:T(8,128)S(1)}, f32[8,32,128]{2,1,0:T(8,128)S(1)}, f32[8,32,128]{2,1,0:T(8,128)S(1)}) custom-call(bf16[2,1024,512]{2,1,0:T(8,128)(2,1)} %bitcast.10, f32[2,1024,512]{2,1,0:T(8,128)} %bitcast.9, f32[2,32,512]{2,1,0:T(8,128)} %bitcast.11), custom_call_target="tpu_custom_call" | custom-call | tf_op jit(solution)/shard_map/left/pallas_call | solution.py:100
  4.4 3.3 %collective-permute-start = (f32[8,32,128]{2,1,0:T(8,128)S(1)}, f32[8,32,128]{2,1,0:T(8,128)S(1)}, u32[]{:S(2)}, u32[]{:S(2)}) collective-permute-start(f32[8,32,128]{2,1,0:T(8,128)S(1)} %get-tuple-element.21), channel_id=1, source_target_pairs={{0,8},{8,0},{16,24},{24,16},{32,40},{40,32},{48,56},{56,48},{64,72... | collective-permute-start | bytes 393224 | tf_op jit(solution)/shard_map/ppermute | solution.py:341
  7.7 1.0 %collective-permute-done.refs_1_ = f32[8,32,128]{2,1,0:T(8,128)S(1)} collective-permute-done((f32[8,32,128]{2,1,0:T(8,128)S(1)}, f32[8,32,128]{2,1,0:T(8,128)S(1)}, u32[]{:S(2)}, u32[]{:S(2)}) %collective-permute-start) | collective-permute-done | bytes 131104 | tf_op jit(solution)/shard_map/ppermute | solution.py:341
  8.7 0.4 collective-permute-start.1
  9.2 1.2 %collective-permute-start.4 = (f32[8,32,128]{2,1,0:T(8,128)S(1)}, f32[8,32,128]{2,1,0:T(8,128)S(1)}, u32[]{:S(2)}, u32[]{:S(2)}) collective-permute-start(f32[8,32,128]{2,1,0:T(8,128)S(1)} %add.3.refs_0_), channel_id=1, source_target_pairs={{0,128},{8,40},{16,144},{24,56},{32,160},{40,8},{48,176},{56,24},{... | collective-permute-start | bytes 393224 | tf_op jit(solution)/shard_map/ppermute | solution.py:341
  10.4 0.8 %collective-permute-start.3 = (f32[8,32,128]{2,1,0:T(8,128)S(1)}, f32[8,32,128]{2,1,0:T(8,128)S(1)}, u32[]{:S(2)}, u32[]{:S(2)}) collective-permute-start(f32[8,32,128]{2,1,0:T(8,128)S(1)} %add.3.refs_0_), channel_id=1, source_target_pairs={{0,192},{8,56},{16,208},{24,40},{32,224},{40,24},{48,240},{56,8},{... | collective-permute-start | bytes 393224 | tf_op jit(solution)/shard_map/ppermute | solution.py:341
  11.1 0.7 collective-permute-start.2
  11.8 3.0 %collective-permute-done.4.refs_3_ = f32[8,32,128]{2,1,0:T(8,128)S(1)} collective-permute-done((f32[8,32,128]{2,1,0:T(8,128)S(1)}, f32[8,32,128]{2,1,0:T(8,128)S(1)}, u32[]{:S(2)}, u32[]{:S(2)}) %collective-permute-start.4) | collective-permute-done | bytes 131104 | tf_op jit(solution)/shard_map/ppermute | solution.py:341
  14.8 1.4 %collective-permute-done.3.refs_2_ = f32[8,32,128]{2,1,0:T(8,128)S(1)} collective-permute-done((f32[8,32,128]{2,1,0:T(8,128)S(1)}, f32[8,32,128]{2,1,0:T(8,128)S(1)}, u32[]{:S(2)}, u32[]{:S(2)}) %collective-permute-start.3) | collective-permute-done | bytes 131104 | tf_op jit(solution)/shard_map/ppermute | solution.py:341
  16.2 0.0 collective-permute-done.2.refs_1_
  16.2 2.0 %collective-permute-start.7 = (f32[8,32,128]{2,1,0:T(8,128)S(1)}, f32[8,32,128]{2,1,0:T(8,128)S(1)}, u32[]{:S(2)}, u32[]{:S(2)}) collective-permute-start(f32[8,32,128]{2,1,0:T(8,128)S(1)} %add.4.refs_0_), channel_id=1, source_target_pairs={{0,32},{8,136},{16,48},{24,152},{32,0},{40,168},{48,16},{56,184},{... | collective-permute-start | bytes 393224 | tf_op jit(solution)/shard_map/ppermute | solution.py:341
  18.2 0.9 %collective-permute-start.6 = (f32[8,32,128]{2,1,0:T(8,128)S(1)}, f32[8,32,128]{2,1,0:T(8,128)S(1)}, u32[]{:S(2)}, u32[]{:S(2)}) collective-permute-start(f32[8,32,128]{2,1,0:T(8,128)S(1)} %add.4.refs_0_), channel_id=1, source_target_pairs={{0,48},{8,200},{16,32},{24,216},{32,16},{40,232},{48,0},{56,248},{... | collective-permute-start | bytes 393224 | tf_op jit(solution)/shard_map/ppermute | solution.py:341
  19.1 2.5 %collective-permute-done.7.refs_3_ = f32[8,32,128]{2,1,0:T(8,128)S(1)} collective-permute-done((f32[8,32,128]{2,1,0:T(8,128)S(1)}, f32[8,32,128]{2,1,0:T(8,128)S(1)}, u32[]{:S(2)}, u32[]{:S(2)}) %collective-permute-start.7) | collective-permute-done | bytes 131104 | tf_op jit(solution)/shard_map/ppermute | solution.py:341
  21.6 1.8 %collective-permute-done.6.refs_2_ = f32[8,32,128]{2,1,0:T(8,128)S(1)} collective-permute-done((f32[8,32,128]{2,1,0:T(8,128)S(1)}, f32[8,32,128]{2,1,0:T(8,128)S(1)}, u32[]{:S(2)}, u32[]{:S(2)}) %collective-permute-start.6) | collective-permute-done | bytes 131104 | tf_op jit(solution)/shard_map/ppermute | solution.py:341
  23.4 0.0 collective-permute-done.5.refs_1_
  23.4 3.0 %collective-permute-start.8 = (f32[8,32,128]{2,1,0:T(8,128)S(1)}, f32[8,32,128]{2,1,0:T(8,128)S(1)}, u32[]{:S(2)}, u32[]{:S(2)}) collective-permute-start(f32[8,32,128]{2,1,0:T(8,128)S(1)} %add.5.p_t), channel_id=1, source_target_pairs={{0,8},{8,0},{16,24},{24,16},{32,40},{40,32},{48,56},{56,48},{64,72... | collective-permute-start | bytes 393224 | tf_op jit(solution)/shard_map/ppermute | solution.py:341
  26.4 0.5 pair.1.pair_terms
  26.9 0.6 right.1
  27.6 10.9 %all_to_all.15.raw = f32[16,8,128]{2,1,0:T(8,128)S(1)} all-to-all(f32[16,8,128]{2,1,0:T(8,128)S(1)} %bitcast.8), channel_id=1, replica_groups={{0,16,32,48,64,80,96,112,128,144,160,176,192,208,224,240},{8,24,40,56,7..., dimensions={0} | all-to-all | bytes 131072 | tf_op jit(solution)/shard_map/all_to_all | solution.py:332
  38.5 0.3 mix.1
  38.8 15.7 %all_to_all.16.x = f32[8,24,128]{2,1,0:T(8,128)S(1)} all-to-all(f32[8,24,128]{2,1,0:T(8,128)S(1)} %mix.1), channel_id=1, replica_groups=mesh['dp'=32,'tensor'=8] {'tensor'}, dimensions={0} | all-to-all | bytes 196608 | tf_op jit(solution)/shard_map/all_to_all | solution.py:332
  54.5 0.7 %unmix.1 = (f32[32,8,128]{2,1,0:T(8,128)S(1)}, f32[2,32,32]{2,1,0:T(8,128)S(1)}) custom-call(f32[8,24,128]{2,1,0:T(8,128)S(1)} %all_to_all.16.x), custom_call_target="tpu_custom_call" | custom-call | tf_op jit(solution)/shard_map/unmix/pallas_call | solution.py:253
  55.2 13.9 %all_to_all.17.raw = f32[32,8,128]{2,1,0:T(8,128)S(1)} all-to-all(f32[32,8,128]{2,1,0:T(8,128)S(1)} %get-tuple-element.31), channel_id=1, replica_groups=mesh['dp'=32,'tensor'=8] {'dp'}, dimensions={0} | all-to-all | bytes 262144 | tf_op jit(solution)/shard_map/all_to_all | solution.py:332
  69.1 3.4 %last.1 = (bf16[2,1024,512]{2,1,0:T(8,128)(2,1)}, f32[2,1024,512]{2,1,0:T(8,128)}, f32[2,32,512]{2,1,0:T(8,128)}) custom-call(bf16[2,2,1024,512]{3,2,1,0:T(8,128)(2,1)S(1)} %get-tuple-element.19.terms, bf16[1024,128]{1,0:T(8,128)(2,1)S(1)} %get-tuple-element.25.p_terms, f32[8,32,128]{2,1,0:T(8,128)S(1)} %collective-permute-done.8.p_other, ...), custom_call_target="tpu_custom_call" | custom-call | tf_op jit(solution)/shard_map/last/pallas_call | solution.py:309
  (6 shorter events, 0.1 us)
Async XLA Ops:
  4.4 4.3 %collective-permute-start = (f32[8,32,128]{2,1,0:T(8,128)S(1)}, f32[8,32,128]{2,1,0:T(8,128)S(1)}, u32[]{:S(2)}, u32[]{:S(2)}) collective-permute-start(f32[8,32,128]{2,1,0:T(8,128)S(1)} %get-tuple-element.21), channel_id=1, source_target_pairs={{0,8},{8,0},{16,24},{24,16},{32,40},{40,32},{48,56},{56,48},{64,72... | collective-permute-start | bytes 393224 | tf_op jit(solution)/shard_map/ppermute | solution.py:341
  8.7 17.7 %collective-permute-start.1 = (f32[1024,512]{1,0:T(8,128)S(1)}, f32[1024,512]{1,0:T(8,128)S(1)}, u32[]{:S(2)}, u32[]{:S(2)}) collective-permute-start(f32[1024,512]{1,0:T(8,128)S(1)} %get-tuple-element.23), channel_id=1, source_target_pairs={{0,8},{8,0},{16,24},{24,16},{32,40},{40,32},{48,56},{56,48},{64,72... | collective-permute-start | bytes 6291464 | tf_op jit(solution)/shard_map/ppermute | solution.py:341
  9.2 5.6 %collective-permute-start.4 = (f32[8,32,128]{2,1,0:T(8,128)S(1)}, f32[8,32,128]{2,1,0:T(8,128)S(1)}, u32[]{:S(2)}, u32[]{:S(2)}) collective-permute-start(f32[8,32,128]{2,1,0:T(8,128)S(1)} %add.3.refs_0_), channel_id=1, source_target_pairs={{0,128},{8,40},{16,144},{24,56},{32,160},{40,8},{48,176},{56,24},{... | collective-permute-start | bytes 393224 | tf_op jit(solution)/shard_map/ppermute | solution.py:341
  10.4 5.8 %collective-permute-start.3 = (f32[8,32,128]{2,1,0:T(8,128)S(1)}, f32[8,32,128]{2,1,0:T(8,128)S(1)}, u32[]{:S(2)}, u32[]{:S(2)}) collective-permute-start(f32[8,32,128]{2,1,0:T(8,128)S(1)} %add.3.refs_0_), channel_id=1, source_target_pairs={{0,192},{8,56},{16,208},{24,40},{32,224},{40,24},{48,240},{56,8},{... | collective-permute-start | bytes 393224 | tf_op jit(solution)/shard_map/ppermute | solution.py:341
  11.1 5.1 %collective-permute-start.2 = (f32[8,32,128]{2,1,0:T(8,128)S(1)}, f32[8,32,128]{2,1,0:T(8,128)S(1)}, u32[]{:S(2)}, u32[]{:S(2)}) collective-permute-start(f32[8,32,128]{2,1,0:T(8,128)S(1)} %add.3.refs_0_), channel_id=1, source_target_pairs={{0,64},{8,24},{16,80},{24,8},{32,96},{40,56},{48,112},{56,40},{64,... | collective-permute-start | bytes 393224 | tf_op jit(solution)/shard_map/ppermute | solution.py:341
  16.2 5.4 %collective-permute-start.7 = (f32[8,32,128]{2,1,0:T(8,128)S(1)}, f32[8,32,128]{2,1,0:T(8,128)S(1)}, u32[]{:S(2)}, u32[]{:S(2)}) collective-permute-start(f32[8,32,128]{2,1,0:T(8,128)S(1)} %add.4.refs_0_), channel_id=1, source_target_pairs={{0,32},{8,136},{16,48},{24,152},{32,0},{40,168},{48,16},{56,184},{... | collective-permute-start | bytes 393224 | tf_op jit(solution)/shard_map/ppermute | solution.py:341
  18.2 5.1 %collective-permute-start.6 = (f32[8,32,128]{2,1,0:T(8,128)S(1)}, f32[8,32,128]{2,1,0:T(8,128)S(1)}, u32[]{:S(2)}, u32[]{:S(2)}) collective-permute-start(f32[8,32,128]{2,1,0:T(8,128)S(1)} %add.4.refs_0_), channel_id=1, source_target_pairs={{0,48},{8,200},{16,32},{24,216},{32,16},{40,232},{48,0},{56,248},{... | collective-permute-start | bytes 393224 | tf_op jit(solution)/shard_map/ppermute | solution.py:341
  19.1 4.3 %collective-permute-start.5 = (f32[8,32,128]{2,1,0:T(8,128)S(1)}, f32[8,32,128]{2,1,0:T(8,128)S(1)}, u32[]{:S(2)}, u32[]{:S(2)}) collective-permute-start(f32[8,32,128]{2,1,0:T(8,128)S(1)} %add.4.refs_0_), channel_id=1, source_target_pairs={{0,16},{8,72},{16,0},{24,88},{32,48},{40,104},{48,32},{56,120},{64... | collective-permute-start | bytes 393224 | tf_op jit(solution)/shard_map/ppermute | solution.py:341
  23.4 4.1 %collective-permute-start.8 = (f32[8,32,128]{2,1,0:T(8,128)S(1)}, f32[8,32,128]{2,1,0:T(8,128)S(1)}, u32[]{:S(2)}, u32[]{:S(2)}) collective-permute-start(f32[8,32,128]{2,1,0:T(8,128)S(1)} %add.5.p_t), channel_id=1, source_target_pairs={{0,8},{8,0},{16,24},{24,16},{32,40},{40,32},{48,56},{56,48},{64,72... | collective-permute-start | bytes 393224 | tf_op jit(solution)/shard_map/ppermute | solution.py:341

commit v9 on v6

--- a/solution.py
+++ b/solution.py
@@ -345,7 +345,7 @@
 
 def sum_axis(total, turn, scale):
     near, wrap, far = (
-        swap(total, lambda x, y, core, to=to: (x ^ to, y, core) if core == turn else (x, y ^ to, core))
+        swap(total, lambda x, y, core, to=to: (x ^ to, y, core) if core != turn else (x, y ^ to, core))
         for to in (1, 3, 2)
     )
     return add([total, near, wrap, far], scale)

time: 72.6 us -> 72.6 us (level)
  no operation moved by 1% of the time
where the time goes in v9:
time: 72.6 us; the launch traced here: 72.4 us
  blocking collectives  40.5 us (56%)
  starting transfers between devices  12.2 us (17%)
  waiting for transfers between devices  9.74 us (13%)
  Pallas kernels  9.33 us (13%)
    all_to_all x3, blocking collectives, exchange(): return lax.all_to_all(x, axis, 0, 0, axis_index_groups=groups, tiled=True)  40.5 us
    ppermute x9, starting transfers between devices, swap(): return lax.ppermute(x, 'dp', pairs)  12.2 us
    ppermute x9, waiting for transfers between devices, swap(): return lax.ppermute(x, 'dp', pairs)  9.74 us
    pallas_call x1, Pallas kernels, left(): pl.pallas_call(left_kernel, in_specs=[pl.BlockSpec(memory_space=pltpu.HBM...  3.64 us
    pallas_call x1, Pallas kernels, last(): pl.pallas_call(last_kernel, in_specs=[whole] * 5, out_specs=[pl.BlockSpec...  3.42 us
  transfers between devices with their start and end apart: 9, of which 5 were waited for; matrix products, arithmetic and copies ran while one was open for 0% of the time, Pallas kernels for 2%

profile of v9, /device:TPU:1, one launch (start us, length us, event | category | flops | bytes accessed | tf_op | source)
XLA Modules:
  0.0 72.4 jit_solution(15041661848422792474)
XLA Ops:
  0.6 3.6 %left.1 = (bf16[2,2,1024,512]{3,2,1,0:T(8,128)(2,1)S(1)}, f32[1024,512]{1,0:T(8,128)S(1)}, f32[8,32,128]{2,1,0:T(8,128)S(1)}, f32[8,32,128]{2,1,0:T(8,128)S(1)}) custom-call(bf16[2,1024,512]{2,1,0:T(8,128)(2,1)} %bitcast.10, f32[2,1024,512]{2,1,0:T(8,128)} %bitcast.9, f32[2,32,512]{2,1,0:T(8,128)} %bitcast.11), custom_call_target="tpu_custom_call" | custom-call | tf_op jit(solution)/shard_map/left/pallas_call | solution.py:98
  4.3 3.3 %collective-permute-start = (f32[8,32,128]{2,1,0:T(8,128)S(1)}, f32[8,32,128]{2,1,0:T(8,128)S(1)}, u32[]{:S(2)}, u32[]{:S(2)}) collective-permute-start(f32[8,32,128]{2,1,0:T(8,128)S(1)} %get-tuple-element.21), channel_id=1, source_target_pairs={{0,8},{8,0},{16,24},{24,16},{32,40},{40,32},{48,56},{56,48},{64,72... | collective-permute-start | bytes 393224 | tf_op jit(solution)/shard_map/ppermute | solution.py:339
  7.6 1.0 %collective-permute-done.refs_1_ = f32[8,32,128]{2,1,0:T(8,128)S(1)} collective-permute-done((f32[8,32,128]{2,1,0:T(8,128)S(1)}, f32[8,32,128]{2,1,0:T(8,128)S(1)}, u32[]{:S(2)}, u32[]{:S(2)}) %collective-permute-start) | collective-permute-done | bytes 131104 | tf_op jit(solution)/shard_map/ppermute | solution.py:339
  8.6 0.4 collective-permute-start.1
  9.1 1.0 %collective-permute-start.4 = (f32[8,32,128]{2,1,0:T(8,128)S(1)}, f32[8,32,128]{2,1,0:T(8,128)S(1)}, u32[]{:S(2)}, u32[]{:S(2)}) collective-permute-start(f32[8,32,128]{2,1,0:T(8,128)S(1)} %add.3.refs_0_), channel_id=1, source_target_pairs={{0,32},{8,136},{16,48},{24,152},{32,0},{40,168},{48,16},{56,184},{... | collective-permute-start | bytes 393224 | tf_op jit(solution)/shard_map/ppermute | solution.py:339
  10.1 0.9 %collective-permute-start.3 = (f32[8,32,128]{2,1,0:T(8,128)S(1)}, f32[8,32,128]{2,1,0:T(8,128)S(1)}, u32[]{:S(2)}, u32[]{:S(2)}) collective-permute-start(f32[8,32,128]{2,1,0:T(8,128)S(1)} %add.3.refs_0_), channel_id=1, source_target_pairs={{0,48},{8,200},{16,32},{24,216},{32,16},{40,232},{48,0},{56,248},{... | collective-permute-start | bytes 393224 | tf_op jit(solution)/shard_map/ppermute | solution.py:339
  10.9 0.8 %collective-permute-start.2 = (f32[8,32,128]{2,1,0:T(8,128)S(1)}, f32[8,32,128]{2,1,0:T(8,128)S(1)}, u32[]{:S(2)}, u32[]{:S(2)}) collective-permute-start(f32[8,32,128]{2,1,0:T(8,128)S(1)} %add.3.refs_0_), channel_id=1, source_target_pairs={{0,16},{8,72},{16,0},{24,88},{32,48},{40,104},{48,32},{56,120},{64... | collective-permute-start | bytes 393224 | tf_op jit(solution)/shard_map/ppermute | solution.py:339
  11.7 3.0 %collective-permute-done.4.refs_3_ = f32[8,32,128]{2,1,0:T(8,128)S(1)} collective-permute-done((f32[8,32,128]{2,1,0:T(8,128)S(1)}, f32[8,32,128]{2,1,0:T(8,128)S(1)}, u32[]{:S(2)}, u32[]{:S(2)}) %collective-permute-start.4) | collective-permute-done | bytes 131104 | tf_op jit(solution)/shard_map/ppermute | solution.py:339
  14.7 1.4 %collective-permute-done.3.refs_2_ = f32[8,32,128]{2,1,0:T(8,128)S(1)} collective-permute-done((f32[8,32,128]{2,1,0:T(8,128)S(1)}, f32[8,32,128]{2,1,0:T(8,128)S(1)}, u32[]{:S(2)}, u32[]{:S(2)}) %collective-permute-start.3) | collective-permute-done | bytes 131104 | tf_op jit(solution)/shard_map/ppermute | solution.py:339
  16.1 0.0 collective-permute-done.2.refs_1_
  16.1 2.0 %collective-permute-start.7 = (f32[8,32,128]{2,1,0:T(8,128)S(1)}, f32[8,32,128]{2,1,0:T(8,128)S(1)}, u32[]{:S(2)}, u32[]{:S(2)}) collective-permute-start(f32[8,32,128]{2,1,0:T(8,128)S(1)} %add.4.refs_0_), channel_id=1, source_target_pairs={{0,128},{8,40},{16,144},{24,56},{32,160},{40,8},{48,176},{56,24},{... | collective-permute-start | bytes 393224 | tf_op jit(solution)/shard_map/ppermute | solution.py:339
  18.1 0.8 %collective-permute-start.6 = (f32[8,32,128]{2,1,0:T(8,128)S(1)}, f32[8,32,128]{2,1,0:T(8,128)S(1)}, u32[]{:S(2)}, u32[]{:S(2)}) collective-permute-start(f32[8,32,128]{2,1,0:T(8,128)S(1)} %add.4.refs_0_), channel_id=1, source_target_pairs={{0,192},{8,56},{16,208},{24,40},{32,224},{40,24},{48,240},{56,8},{... | collective-permute-start | bytes 393224 | tf_op jit(solution)/shard_map/ppermute | solution.py:339
  18.9 2.6 %collective-permute-done.7.refs_3_ = f32[8,32,128]{2,1,0:T(8,128)S(1)} collective-permute-done((f32[8,32,128]{2,1,0:T(8,128)S(1)}, f32[8,32,128]{2,1,0:T(8,128)S(1)}, u32[]{:S(2)}, u32[]{:S(2)}) %collective-permute-start.7) | collective-permute-done | bytes 131104 | tf_op jit(solution)/shard_map/ppermute | solution.py:339
  21.5 1.8 %collective-permute-done.6.refs_2_ = f32[8,32,128]{2,1,0:T(8,128)S(1)} collective-permute-done((f32[8,32,128]{2,1,0:T(8,128)S(1)}, f32[8,32,128]{2,1,0:T(8,128)S(1)}, u32[]{:S(2)}, u32[]{:S(2)}) %collective-permute-start.6) | collective-permute-done | bytes 131104 | tf_op jit(solution)/shard_map/ppermute | solution.py:339
  23.3 0.0 collective-permute-done.5.refs_1_
  23.3 3.0 %collective-permute-start.8 = (f32[8,32,128]{2,1,0:T(8,128)S(1)}, f32[8,32,128]{2,1,0:T(8,128)S(1)}, u32[]{:S(2)}, u32[]{:S(2)}) collective-permute-start(f32[8,32,128]{2,1,0:T(8,128)S(1)} %add.5.p_t), channel_id=1, source_target_pairs={{0,8},{8,0},{16,24},{24,16},{32,40},{40,32},{48,56},{56,48},{64,72... | collective-permute-start | bytes 393224 | tf_op jit(solution)/shard_map/ppermute | solution.py:339
  26.3 0.5 pair.1.pair_terms
  26.8 0.6 right.1
  27.5 10.9 %all_to_all.15.raw = f32[16,8,128]{2,1,0:T(8,128)S(1)} all-to-all(f32[16,8,128]{2,1,0:T(8,128)S(1)} %bitcast.8), channel_id=1, replica_groups={{0,16,32,48,64,80,96,112,128,144,160,176,192,208,224,240},{8,24,40,56,7..., dimensions={0} | all-to-all | bytes 131072 | tf_op jit(solution)/shard_map/all_to_all | solution.py:330
  38.4 0.3 mix.1
  38.7 15.7 %all_to_all.16.x = f32[8,24,128]{2,1,0:T(8,128)S(1)} all-to-all(f32[8,24,128]{2,1,0:T(8,128)S(1)} %mix.1), channel_id=1, replica_groups=mesh['dp'=32,'tensor'=8] {'tensor'}, dimensions={0} | all-to-all | bytes 196608 | tf_op jit(solution)/shard_map/all_to_all | solution.py:330
  54.3 0.7 %unmix.1 = (f32[32,8,128]{2,1,0:T(8,128)S(1)}, f32[2,32,32]{2,1,0:T(8,128)S(1)}) custom-call(f32[8,24,128]{2,1,0:T(8,128)S(1)} %all_to_all.16.x), custom_call_target="tpu_custom_call" | custom-call | tf_op jit(solution)/shard_map/unmix/pallas_call | solution.py:251
  55.1 13.9 %all_to_all.17.raw = f32[32,8,128]{2,1,0:T(8,128)S(1)} all-to-all(f32[32,8,128]{2,1,0:T(8,128)S(1)} %get-tuple-element.31), channel_id=1, replica_groups=mesh['dp'=32,'tensor'=8] {'dp'}, dimensions={0} | all-to-all | bytes 262144 | tf_op jit(solution)/shard_map/all_to_all | solution.py:330
  69.0 3.4 %last.1 = (bf16[2,1024,512]{2,1,0:T(8,128)(2,1)}, f32[2,1024,512]{2,1,0:T(8,128)}, f32[2,32,512]{2,1,0:T(8,128)}) custom-call(bf16[2,2,1024,512]{3,2,1,0:T(8,128)(2,1)S(1)} %get-tuple-element.19.terms, bf16[1024,128]{1,0:T(8,128)(2,1)S(1)} %get-tuple-element.25.p_terms, f32[8,32,128]{2,1,0:T(8,128)S(1)} %collective-permute-done.8.p_other, ...), custom_call_target="tpu_custom_call" | custom-call | tf_op jit(solution)/shard_map/last/pallas_call | solution.py:307
  (6 shorter events, 0.1 us)
Async XLA Ops:
  4.3 4.3 %collective-permute-start = (f32[8,32,128]{2,1,0:T(8,128)S(1)}, f32[8,32,128]{2,1,0:T(8,128)S(1)}, u32[]{:S(2)}, u32[]{:S(2)}) collective-permute-start(f32[8,32,128]{2,1,0:T(8,128)S(1)} %get-tuple-element.21), channel_id=1, source_target_pairs={{0,8},{8,0},{16,24},{24,16},{32,40},{40,32},{48,56},{56,48},{64,72... | collective-permute-start | bytes 393224 | tf_op jit(solution)/shard_map/ppermute | solution.py:339
  8.6 17.7 %collective-permute-start.1 = (f32[1024,512]{1,0:T(8,128)S(1)}, f32[1024,512]{1,0:T(8,128)S(1)}, u32[]{:S(2)}, u32[]{:S(2)}) collective-permute-start(f32[1024,512]{1,0:T(8,128)S(1)} %get-tuple-element.23), channel_id=1, source_target_pairs={{0,8},{8,0},{16,24},{24,16},{32,40},{40,32},{48,56},{56,48},{64,72... | collective-permute-start | bytes 6291464 | tf_op jit(solution)/shard_map/ppermute | solution.py:339
  9.1 5.6 %collective-permute-start.4 = (f32[8,32,128]{2,1,0:T(8,128)S(1)}, f32[8,32,128]{2,1,0:T(8,128)S(1)}, u32[]{:S(2)}, u32[]{:S(2)}) collective-permute-start(f32[8,32,128]{2,1,0:T(8,128)S(1)} %add.3.refs_0_), channel_id=1, source_target_pairs={{0,32},{8,136},{16,48},{24,152},{32,0},{40,168},{48,16},{56,184},{... | collective-permute-start | bytes 393224 | tf_op jit(solution)/shard_map/ppermute | solution.py:339
  10.1 6.0 %collective-permute-start.3 = (f32[8,32,128]{2,1,0:T(8,128)S(1)}, f32[8,32,128]{2,1,0:T(8,128)S(1)}, u32[]{:S(2)}, u32[]{:S(2)}) collective-permute-start(f32[8,32,128]{2,1,0:T(8,128)S(1)} %add.3.refs_0_), channel_id=1, source_target_pairs={{0,48},{8,200},{16,32},{24,216},{32,16},{40,232},{48,0},{56,248},{... | collective-permute-start | bytes 393224 | tf_op jit(solution)/shard_map/ppermute | solution.py:339
  10.9 5.2 %collective-permute-start.2 = (f32[8,32,128]{2,1,0:T(8,128)S(1)}, f32[8,32,128]{2,1,0:T(8,128)S(1)}, u32[]{:S(2)}, u32[]{:S(2)}) collective-permute-start(f32[8,32,128]{2,1,0:T(8,128)S(1)} %add.3.refs_0_), channel_id=1, source_target_pairs={{0,16},{8,72},{16,0},{24,88},{32,48},{40,104},{48,32},{56,120},{64... | collective-permute-start | bytes 393224 | tf_op jit(solution)/shard_map/ppermute | solution.py:339
  16.1 5.4 %collective-permute-start.7 = (f32[8,32,128]{2,1,0:T(8,128)S(1)}, f32[8,32,128]{2,1,0:T(8,128)S(1)}, u32[]{:S(2)}, u32[]{:S(2)}) collective-permute-start(f32[8,32,128]{2,1,0:T(8,128)S(1)} %add.4.refs_0_), channel_id=1, source_target_pairs={{0,128},{8,40},{16,144},{24,56},{32,160},{40,8},{48,176},{56,24},{... | collective-permute-start | bytes 393224 | tf_op jit(solution)/shard_map/ppermute | solution.py:339
  18.1 5.1 %collective-permute-start.6 = (f32[8,32,128]{2,1,0:T(8,128)S(1)}, f32[8,32,128]{2,1,0:T(8,128)S(1)}, u32[]{:S(2)}, u32[]{:S(2)}) collective-permute-start(f32[8,32,128]{2,1,0:T(8,128)S(1)} %add.4.refs_0_), channel_id=1, source_target_pairs={{0,192},{8,56},{16,208},{24,40},{32,224},{40,24},{48,240},{56,8},{... | collective-permute-start | bytes 393224 | tf_op jit(solution)/shard_map/ppermute | solution.py:339
  18.9 4.4 %collective-permute-start.5 = (f32[8,32,128]{2,1,0:T(8,128)S(1)}, f32[8,32,128]{2,1,0:T(8,128)S(1)}, u32[]{:S(2)}, u32[]{:S(2)}) collective-permute-start(f32[8,32,128]{2,1,0:T(8,128)S(1)} %add.4.refs_0_), channel_id=1, source_target_pairs={{0,64},{8,24},{16,80},{24,8},{32,96},{40,56},{48,112},{56,40},{64,... | collective-permute-start | bytes 393224 | tf_op jit(solution)/shard_map/ppermute | solution.py:339
  23.3 4.1 %collective-permute-start.8 = (f32[8,32,128]{2,1,0:T(8,128)S(1)}, f32[8,32,128]{2,1,0:T(8,128)S(1)}, u32[]{:S(2)}, u32[]{:S(2)}) collective-permute-start(f32[8,32,128]{2,1,0:T(8,128)S(1)} %add.5.p_t), channel_id=1, source_target_pairs={{0,8},{8,0},{16,24},{24,16},{32,40},{40,32},{48,56},{56,48},{64,72... | collective-permute-start | bytes 393224 | tf_op jit(solution)/shard_map/ppermute | solution.py:339
